TPU v7x, 768 devices: a whole 4x8x12 slice. The times are simulated.
768 devices in a mesh: gx: 8 (over y_lo, core), gy: 96 (over z, y_hi, x).
Axes of the slice: x: 4, y: 8 (y_hi: 2, y_lo: 4; y = y_hi * 4 + y_lo), z: 12, core: 2. Of those that a mesh axis runs over, the one named last changes fastest.
Arguments:
- electric_field: float32 [2, 3, 128, 1536, 128], P(None, None, 'gx', 'gy'), may hold values from -6 to 6
- magnetic_field: float32 [2, 3, 128, 1536, 128], P(None, None, 'gx', 'gy'), may hold values from -6 to 6
- material: int32 [128, 1536, 128], P('gx', 'gy'), may hold values from 0 to 7
- absorber_mask: int32 [128, 1536, 128], P('gx', 'gy'), may hold values 0 or 1
- permittivity: float32 [8], replicated, may hold values from 1 to 12
- conductivity: float32 [8], replicated, may hold values from 0 to 0.6
- bloch_phase: float32 [2], replicated, may hold values from -3.140625 to 3.140625
Outputs:
- electric_next: float32 [2, 3, 128, 1536, 128], P(None, None, 'gx', 'gy')
- magnetic_next: float32 [2, 3, 128, 1536, 128], P(None, None, 'gx', 'gy')
Inputs may be any that keep to these rules, and one draw needn't show every extreme that they name: Every entry of `material` is an index from 0 to 7 into `permittivity` and `conductivity`.
All inputs are finite; a program needn't handle non-finite values. No bound on the sum of `absorber_mask` on one device may be relied on, other than what follows from the above.
Results may differ from a plain program's by a relative error of at most 0.00002.
Values sent between devices are 32-bit elements; how exact they have to be, the bound alone decides.
No kernel may reach another device: no remote copies, remote signals or barrier semaphores. Data moves between devices by JAX's collectives and lax.ppermute only.
A program may use at most 32 MiB of HBM per device.

v0:
```python
import jax
import jax.numpy as jnp
from jax import lax
from jax.sharding import PartitionSpec as P

NZ = 128
STEPS = 4
ABSORB = 10


TIME_STEP = 0.55
ABSORB_PEAK = 1.5


def shifted(value, axis, steps):
    count = lax.axis_size(axis)
    pairs = [(source, (source + steps) % count) for source in range(count)]
    return lax.ppermute(value, axis, pairs)


def rotate(complex_pair, turning):
    cosine_part = jnp.cos(turning)
    sine_part = jnp.sin(turning)
    return jnp.stack(
        [
            complex_pair[0] * cosine_part - complex_pair[1] * sine_part,
            complex_pair[0] * sine_part + complex_pair[1] * cosine_part,
        ]
    )


def ahead_depth(values):
    return jnp.concatenate([values[..., 1:], jnp.zeros_like(values[..., :1])], -1)


def behind_depth(values):
    return jnp.concatenate([jnp.zeros_like(values[..., :1]), values[..., :-1]], -1)


def step_magnetic(electric, magnetic, decay, push, east_side, north_side):
    first_field, second_field, third_field = (electric[:, 0], electric[:, 1], electric[:, 2])
    curl_first = north_side[:, 1] - third_field - (ahead_depth(second_field) - second_field)
    curl_second = ahead_depth(first_field) - first_field - (east_side[:, 1] - third_field)
    curl_third = east_side[:, 0] - second_field - (north_side[:, 0] - first_field)
    curl_all = jnp.stack([curl_first, curl_second, curl_third], 1)
    return decay * magnetic - push * curl_all


def step_electric(electric, magnetic, scale, drive, west_side, south_side):
    first_field, second_field, third_field = (magnetic[:, 0], magnetic[:, 1], magnetic[:, 2])
    curl_first = third_field - south_side[:, 1] - (second_field - behind_depth(second_field))
    curl_second = first_field - behind_depth(first_field) - (third_field - west_side[:, 1])
    curl_third = second_field - west_side[:, 0] - (first_field - south_side[:, 0])
    curl_all = jnp.stack([curl_first, curl_second, curl_third], 1)
    return scale * electric + drive * curl_all


def lookup(values_table, codes):
    result = jnp.zeros(codes.shape, jnp.float32)
    for table_row in range(values_table.shape[0]):
        result = jnp.where(codes == table_row, values_table[table_row], result)
    return result


def coefficients(permittivity_cells, conductivity_cells, mask_cells):
    positions = jnp.arange(NZ).astype(jnp.float32)
    reach_depth = (
        jnp.maximum(jnp.maximum(ABSORB - positions, positions - (NZ - 1 - ABSORB)), 0.0) / ABSORB
    )
    profile = reach_depth * reach_depth * reach_depth
    magnetic_loss = mask_cells.astype(jnp.float32) * (ABSORB_PEAK * profile)
    electric_loss = conductivity_cells + magnetic_loss
    half_loss = electric_loss * (TIME_STEP / 2.0) / permittivity_cells
    scale = (1.0 - half_loss) / (1.0 + half_loss)
    drive = TIME_STEP / (permittivity_cells * (1.0 + half_loss))
    half_magnetic = magnetic_loss * (TIME_STEP / 2.0)
    decay = (1.0 - half_magnetic) / (1.0 + half_magnetic)
    push = TIME_STEP / (1.0 + half_magnetic)
    return (scale, drive, decay, push)


def per_device(
    electric_field, magnetic_field, material, absorber_mask, permittivity, conductivity, bloch_phase
):
    index_first = lax.axis_index("gx")
    index_second = lax.axis_index("gy")
    count_first = lax.axis_size("gx")
    count_second = lax.axis_size("gy")
    electric = electric_field
    magnetic = magnetic_field
    scale, drive, decay, push = coefficients(
        lookup(permittivity, material), lookup(conductivity, material), absorber_mask
    )
    turn_east = jnp.where(index_first == count_first - 1, bloch_phase[0], 0.0)
    turn_north = jnp.where(index_second == count_second - 1, bloch_phase[1], 0.0)
    turn_west = jnp.where(index_first == 0, -bloch_phase[0], 0.0)
    turn_south = jnp.where(index_second == 0, -bloch_phase[1], 0.0)
    for repeat in range(STEPS):
        east_face = shifted(electric[:, 1:3, :1], "gx", -1)
        north_face = shifted(electric[:, ::2, :, :1], "gy", -1)
        east_side = jnp.concatenate([electric[:, 1:3, 1:], rotate(east_face, turn_east)], 2)
        north_side = jnp.concatenate([electric[:, ::2, :, 1:], rotate(north_face, turn_north)], 3)
        magnetic = step_magnetic(electric, magnetic, decay, push, east_side, north_side)
        west_face = shifted(magnetic[:, 1:3, -1:], "gx", 1)
        south_face = shifted(magnetic[:, ::2, :, -1:], "gy", 1)
        west_side = jnp.concatenate([rotate(west_face, turn_west), magnetic[:, 1:3, :-1]], 2)
        south_side = jnp.concatenate([rotate(south_face, turn_south), magnetic[:, ::2, :, :-1]], 3)
        electric = step_electric(electric, magnetic, scale, drive, west_side, south_side)
    return (electric, magnetic)


def solution(mesh):
    in_specs = (
        P(None, None, "gx", "gy", None),
        P(None, None, "gx", "gy", None),
        P("gx", "gy", None),
        P("gx", "gy", None),
        P(),
        P(),
        P(),
    )
    out_specs = (P(None, None, "gx", "gy", None), P(None, None, "gx", "gy", None))
    return jax.shard_map(
        per_device, mesh=mesh, in_specs=in_specs, out_specs=out_specs, check_vma=False
    )
```

profile of v0, /device:TPU:25, one launch (start us, length us, event | category | flops | bytes accessed | tf_op | source)
XLA Modules:
  0.0 154.5 jit_solution(16920054894085524516)
XLA Ops:
  0.6 0.8 slice.524
  1.4 2.6 %collective-permute-start.1 = (f32[2,2,1,16,128]{4,2,3,0,1:T(1,128)S(1)}, f32[2,2,1,16,128]{4,2,3,0,1:T(1,128)S(1)}, u32[]{:S(2)}, u32[]{:S(2)}) collective-permute-start(f32[2,2,1,16,128]{4,2,3,0,1:T(1,128)S(1)} %copy.103), channel_id=1, source_target_pairs={{0,672},{96,0},{192,96},{288,192},{384,288},{480,384},{576,480},{6... | collective-permute-start | bytes 98312 | tf_op jit(solution)/shard_map/ppermute | solution.py:18
  4.0 1.0 slice.513
  5.0 19.1 %collective-permute-start = (f32[2,2,16,1,128]{4,2,3,0,1:T(8,128)S(1)}, f32[2,2,16,1,128]{4,2,3,0,1:T(8,128)S(1)}, u32[]{:S(2)}, u32[]{:S(2)}) collective-permute-start(f32[2,2,16,1,128]{4,2,3,0,1:T(8,128)S(1)} %copy.193), channel_id=1, source_target_pairs={{0,95},{1,0},{2,1},{3,2},{4,3},{5,4},{6,5},{7,6},{8,7},{9,8},{10,9... | collective-permute-start | bytes 98312 | tf_op jit(solution)/shard_map/ppermute | solution.py:18
  24.2 1.9 %fusion.100 = (f32[2,1,16,16,128]{4,3,2,1,0:T(8,128)}, f32[2,1,16,16,128]{4,3,2,1,0:T(8,128)S(1)}) fusion(f32[2,3,16,16,128]{4,3,2,1,0:T(8,128)} %param.7), kind=kLoop, calls=%fused_computation.236 | loop fusion | bytes 1048576 | tf_op jit(solution)/shard_map/slice | solution.py:41
  26.0 0.7 fusion.102
  26.7 0.7 fusion.101
  27.4 11.0 %subtract_divide_fusion.1 = (f32[16,16,128]{2,1,0:T(8,128)}, pred[16,16,128]{2,1,0:T(8,128)(4,1)}, pred[16,16,128]{2,1,0:T(8,128)(4,1)}, pred[16,16,128]{2,1,0:T...) fusion(f32[]{:T(128)} %bitcast.15, f32[]{:T(128)} %bitcast.14, ...), kind=kLoop, calls=%fused_computation.170 | loop fusion | flops 1212416 | bytes 918080 | tf_op jit(solution)/shard_map/div | solution.py:74
  38.4 0.6 fusion.103
  40.6 0.2 copy.88
  40.9 0.2 copy.196
  41.0 0.2 copy.192
  41.3 0.1 slice.653
  41.9 0.1 slice.655
  42.0 0.8 copy-done.2
  42.8 0.2 fusion.89
  43.0 0.9 copy-done.1
  44.0 0.3 fusion
  44.3 0.6 slice.532
  44.9 1.9 %collective-permute-start.2 = (f32[2,2,16,1,128]{4,2,3,1,0:T(8,128)}, f32[2,2,16,1,128]{4,2,3,1,0:T(8,128)}, u32[]{:S(2)}, u32[]{:S(2)}) collective-permute-start(f32[2,2,16,1,128]{4,2,3,1,0:T(8,128)} %slice.532), channel_id=1, source_target_pairs={{0,1},{1,2},{2,3},{3,4},{4,5},{5,6},{6,7},{7,8},{8,9},{9,10},{10,1... | collective-permute-start | bytes 98312 | tf_op jit(solution)/shard_map/ppermute | solution.py:18
  46.9 10.8 %multiply_divide_fusion = f32[16,16,128]{2,1,0:T(8,128)} fusion(pred[16,16,128]{2,1,0:T(8,128)(4,1)S(1)} %copy-done.13, pred[16,16,128]{2,1,0:T(8,128)(4,1)S(1)} %copy-done.12, pred[16,16,128]{2,1,0:T(8,128)(4,1)S(1)} %copy-done.11, pred[16,16,128]{2,1,0:T(8,128)(4,1)S(1)} %copy-done.10, pred[16,16,128]{2,1,0:T(8,128)(4,1)S(1)} %copy-done.9, ...), kind=kLoop, calls=%fused_computation.169 | loop fusion | flops 786432 | bytes 524864 | tf_op jit(solution)/shard_map/div | solution.py:75
  59.2 1.0 copy.87
  60.4 5.1 %collective-permute-start.3 = (f32[2,2,1,16,128]{4,2,3,0,1:T(1,128)S(1)}, f32[2,2,1,16,128]{4,2,3,0,1:T(1,128)S(1)}, u32[]{:S(2)}, u32[]{:S(2)}) collective-permute-start(f32[2,2,1,16,128]{4,2,3,0,1:T(1,128)S(1)} %copy.201), channel_id=1, source_target_pairs={{0,96},{96,192},{192,288},{288,384},{384,480},{480,576},{576,672},... | collective-permute-start | bytes 98312 | tf_op jit(solution)/shard_map/ppermute | solution.py:18
  65.5 0.7 multiply_subtract_fusion.11
  66.3 0.2 collective-permute-done.3
  66.6 0.3 fusion.80
  66.9 0.3 fusion.1
  67.2 11.8 %collective-permute-start.4 = (f32[2,2,16,1,128]{4,2,3,0,1:T(8,128)S(1)}, f32[2,2,16,1,128]{4,2,3,0,1:T(8,128)S(1)}, u32[]{:S(2)}, u32[]{:S(2)}) collective-permute-start(f32[2,2,16,1,128]{4,2,3,0,1:T(8,128)S(1)} %copy.204), channel_id=1, source_target_pairs={{0,95},{1,0},{2,1},{3,2},{4,3},{5,4},{6,5},{7,6},{8,7},{9,8},{10,9... | collective-permute-start | bytes 98312 | tf_op jit(solution)/shard_map/ppermute | solution.py:18
  79.1 2.4 %collective-permute-start.5 = (f32[2,2,1,16,128]{4,2,3,1,0:T(1,128)S(1)}, f32[2,2,1,16,128]{4,2,3,1,0:T(1,128)S(1)}, u32[]{:S(2)}, u32[]{:S(2)}) collective-permute-start(f32[2,2,1,16,128]{4,2,3,1,0:T(1,128)S(1)} %slice.685), channel_id=1, source_target_pairs={{0,672},{96,0},{192,96},{288,192},{384,288},{480,384},{576,480},{6... | collective-permute-start | bytes 98312 | tf_op jit(solution)/shard_map/ppermute | solution.py:18
  81.6 5.4 %collective-permute-done.5 = f32[2,2,1,16,128]{4,2,3,1,0:T(1,128)S(1)} collective-permute-done((f32[2,2,1,16,128]{4,2,3,1,0:T(1,128)S(1)}, f32[2,2,1,16,128]{4,2,3,1,0:T(1,128)S(1)}, u32[]{:S(2)}, u32[]{:S(2)}) %collective-permute-start.5) | collective-permute-done | bytes 32800 | tf_op jit(solution)/shard_map/ppermute | solution.py:18
  87.1 0.1 slice.681
  87.3 0.1 slice.683
  87.4 0.1 fusion.72
  87.5 0.4 fusion.2
  88.0 1.9 %collective-permute-start.7 = (f32[2,2,1,16,128]{4,2,3,0,1:T(1,128)S(1)}, f32[2,2,1,16,128]{4,2,3,0,1:T(1,128)S(1)}, u32[]{:S(2)}, u32[]{:S(2)}) collective-permute-start(f32[2,2,1,16,128]{4,2,3,0,1:T(1,128)S(1)} %copy.212), channel_id=1, source_target_pairs={{0,96},{96,192},{192,288},{288,384},{384,480},{480,576},{576,672},... | collective-permute-start | bytes 98312 | tf_op jit(solution)/shard_map/ppermute | solution.py:18
  90.0 1.9 %collective-permute-start.6 = (f32[2,2,16,1,128]{4,2,3,1,0:T(8,128)S(1)}, f32[2,2,16,1,128]{4,2,3,1,0:T(8,128)S(1)}, u32[]{:S(2)}, u32[]{:S(2)}) collective-permute-start(f32[2,2,16,1,128]{4,2,3,1,0:T(8,128)S(1)} %slice.566), channel_id=1, source_target_pairs={{0,1},{1,2},{2,3},{3,4},{4,5},{5,6},{6,7},{7,8},{8,9},{9,10},{10,1... | collective-permute-start | bytes 98312 | tf_op jit(solution)/shard_map/ppermute | solution.py:18
  92.0 10.7 %collective-permute-done.6 = f32[2,2,16,1,128]{4,2,3,1,0:T(8,128)S(1)} collective-permute-done((f32[2,2,16,1,128]{4,2,3,1,0:T(8,128)S(1)}, f32[2,2,16,1,128]{4,2,3,1,0:T(8,128)S(1)}, u32[]{:S(2)}, u32[]{:S(2)}) %collective-permute-start.6) | collective-permute-done | bytes 32800 | tf_op jit(solution)/shard_map/ppermute | solution.py:18
  102.9 0.3 fusion.63
  103.1 0.4 fusion.3
  103.6 2.0 %collective-permute-start.8 = (f32[2,2,16,1,128]{4,2,3,0,1:T(8,128)S(1)}, f32[2,2,16,1,128]{4,2,3,0,1:T(8,128)S(1)}, u32[]{:S(2)}, u32[]{:S(2)}) collective-permute-start(f32[2,2,16,1,128]{4,2,3,0,1:T(8,128)S(1)} %copy.215), channel_id=1, source_target_pairs={{0,95},{1,0},{2,1},{3,2},{4,3},{5,4},{6,5},{7,6},{8,7},{9,8},{10,9... | collective-permute-start | bytes 98312 | tf_op jit(solution)/shard_map/ppermute | solution.py:18
  105.6 3.5 %collective-permute-start.9 = (f32[2,2,1,16,128]{4,2,3,1,0:T(1,128)S(1)}, f32[2,2,1,16,128]{4,2,3,1,0:T(1,128)S(1)}, u32[]{:S(2)}, u32[]{:S(2)}) collective-permute-start(f32[2,2,1,16,128]{4,2,3,1,0:T(1,128)S(1)} %slice.715), channel_id=1, source_target_pairs={{0,672},{96,0},{192,96},{288,192},{384,288},{480,384},{576,480},{6... | collective-permute-start | bytes 98312 | tf_op jit(solution)/shard_map/ppermute | solution.py:18
  109.2 3.5 %collective-permute-done.9 = f32[2,2,1,16,128]{4,2,3,1,0:T(1,128)S(1)} collective-permute-done((f32[2,2,1,16,128]{4,2,3,1,0:T(1,128)S(1)}, f32[2,2,1,16,128]{4,2,3,1,0:T(1,128)S(1)}, u32[]{:S(2)}, u32[]{:S(2)}) %collective-permute-start.9) | collective-permute-done | bytes 32800 | tf_op jit(solution)/shard_map/ppermute | solution.py:18
  112.9 0.1 slice.711
  113.0 0.1 slice.713
  113.1 0.1 fusion.55
  113.3 0.5 fusion.4
  113.8 1.9 %collective-permute-start.11 = (f32[2,2,1,16,128]{4,2,3,0,1:T(1,128)S(1)}, f32[2,2,1,16,128]{4,2,3,0,1:T(1,128)S(1)}, u32[]{:S(2)}, u32[]{:S(2)}) collective-permute-start(f32[2,2,1,16,128]{4,2,3,0,1:T(1,128)S(1)} %copy.223), channel_id=1, source_target_pairs={{0,96},{96,192},{192,288},{288,384},{384,480},{480,576},{576,672},... | collective-permute-start | bytes 98312 | tf_op jit(solution)/shard_map/ppermute | solution.py:18
  115.8 3.3 %collective-permute-start.10 = (f32[2,2,16,1,128]{4,2,3,1,0:T(8,128)S(1)}, f32[2,2,16,1,128]{4,2,3,1,0:T(8,128)S(1)}, u32[]{:S(2)}, u32[]{:S(2)}) collective-permute-start(f32[2,2,16,1,128]{4,2,3,1,0:T(8,128)S(1)} %slice.600), channel_id=1, source_target_pairs={{0,1},{1,2},{2,3},{3,4},{4,5},{5,6},{6,7},{7,8},{8,9},{9,10},{10,1... | collective-permute-start | bytes 98312 | tf_op jit(solution)/shard_map/ppermute | solution.py:18
  119.2 9.4 %collective-permute-done.10 = f32[2,2,16,1,128]{4,2,3,1,0:T(8,128)S(1)} collective-permute-done((f32[2,2,16,1,128]{4,2,3,1,0:T(8,128)S(1)}, f32[2,2,16,1,128]{4,2,3,1,0:T(8,128)S(1)}, u32[]{:S(2)}, u32[]{:S(2)}) %collective-permute-start.10) | collective-permute-done | bytes 32800 | tf_op jit(solution)/shard_map/ppermute | solution.py:18
  128.7 0.2 fusion.46
  128.9 0.4 fusion.5
  129.4 1.9 %collective-permute-start.12 = (f32[2,2,16,1,128]{4,2,3,1,0:T(8,128)S(1)}, f32[2,2,16,1,128]{4,2,3,1,0:T(8,128)S(1)}, u32[]{:S(2)}, u32[]{:S(2)}) collective-permute-start(f32[2,2,16,1,128]{4,2,3,1,0:T(8,128)S(1)} %slice.617), channel_id=1, source_target_pairs={{0,95},{1,0},{2,1},{3,2},{4,3},{5,4},{6,5},{7,6},{8,7},{9,8},{10,9... | collective-permute-start | bytes 98312 | tf_op jit(solution)/shard_map/ppermute | solution.py:18
  131.5 3.6 %collective-permute-start.13 = (f32[2,2,1,16,128]{4,2,3,1,0:T(1,128)S(1)}, f32[2,2,1,16,128]{4,2,3,1,0:T(1,128)S(1)}, u32[]{:S(2)}, u32[]{:S(2)}) collective-permute-start(f32[2,2,1,16,128]{4,2,3,1,0:T(1,128)S(1)} %slice.745), channel_id=1, source_target_pairs={{0,672},{96,0},{192,96},{288,192},{384,288},{480,384},{576,480},{6... | collective-permute-start | bytes 98312 | tf_op jit(solution)/shard_map/ppermute | solution.py:18
  135.1 3.4 %collective-permute-done.13 = f32[2,2,1,16,128]{4,2,3,1,0:T(1,128)S(1)} collective-permute-done((f32[2,2,1,16,128]{4,2,3,1,0:T(1,128)S(1)}, f32[2,2,1,16,128]{4,2,3,1,0:T(1,128)S(1)}, u32[]{:S(2)}, u32[]{:S(2)}) %collective-permute-start.13) | collective-permute-done | bytes 32800 | tf_op jit(solution)/shard_map/ppermute | solution.py:18
  138.7 0.1 slice.741
  138.8 0.1 slice.743
  139.1 0.5 fusion.6
  139.6 3.4 %collective-permute-start.14 = (f32[2,2,16,1,128]{4,2,3,1,0:T(8,128)S(1)}, f32[2,2,16,1,128]{4,2,3,1,0:T(8,128)S(1)}, u32[]{:S(2)}, u32[]{:S(2)}) collective-permute-start(f32[2,2,16,1,128]{4,2,3,1,0:T(8,128)S(1)} %slice.634), channel_id=1, source_target_pairs={{0,1},{1,2},{2,3},{3,4},{4,5},{5,6},{6,7},{7,8},{8,9},{9,10},{10,1... | collective-permute-start | bytes 98312 | tf_op jit(solution)/shard_map/ppermute | solution.py:18
  143.1 1.1 copy.191
  144.2 2.2 %collective-permute-start.15 = (f32[2,2,1,16,128]{4,2,3,0,1:T(1,128)S(1)}, f32[2,2,1,16,128]{4,2,3,0,1:T(1,128)S(1)}, u32[]{:S(2)}, u32[]{:S(2)}) collective-permute-start(f32[2,2,1,16,128]{4,2,3,0,1:T(1,128)S(1)} %copy.233), channel_id=1, source_target_pairs={{0,96},{96,192},{192,288},{288,384},{384,480},{480,576},{576,672},... | collective-permute-start | bytes 98312 | tf_op jit(solution)/shard_map/ppermute | solution.py:18
  146.4 6.0 %collective-permute-done.14 = f32[2,2,16,1,128]{4,2,3,1,0:T(8,128)S(1)} collective-permute-done((f32[2,2,16,1,128]{4,2,3,1,0:T(8,128)S(1)}, f32[2,2,16,1,128]{4,2,3,1,0:T(8,128)S(1)}, u32[]{:S(2)}, u32[]{:S(2)}) %collective-permute-start.14) | collective-permute-done | bytes 32800 | tf_op jit(solution)/shard_map/ppermute | solution.py:18
  152.6 0.3 fusion.27
  152.9 0.5 fusion.7
  153.4 1.1 copy.190
  (116 shorter events, 2.9 us)
Async XLA Ops:
  1.4 40.1 %collective-permute-start.1 = (f32[2,2,1,16,128]{4,2,3,0,1:T(1,128)S(1)}, f32[2,2,1,16,128]{4,2,3,0,1:T(1,128)S(1)}, u32[]{:S(2)}, u32[]{:S(2)}) collective-permute-start(f32[2,2,1,16,128]{4,2,3,0,1:T(1,128)S(1)} %copy.103), channel_id=1, source_target_pairs={{0,672},{96,0},{192,96},{288,192},{384,288},{480,384},{576,480},{6... | collective-permute-start | bytes 98312 | tf_op jit(solution)/shard_map/ppermute | solution.py:18
  5.0 21.0 %copy-start.14 = (f32[8]{0:T(128)S(1)}, f32[8]{0:T(128)}, u32[]{:S(2)}) copy-start(f32[8]{0:T(128)} %param.11) | copy-start | bytes 100
  5.0 36.5 %collective-permute-start = (f32[2,2,16,1,128]{4,2,3,0,1:T(8,128)S(1)}, f32[2,2,16,1,128]{4,2,3,0,1:T(8,128)S(1)}, u32[]{:S(2)}, u32[]{:S(2)}) collective-permute-start(f32[2,2,16,1,128]{4,2,3,0,1:T(8,128)S(1)} %copy.193), channel_id=1, source_target_pairs={{0,95},{1,0},{2,1},{3,2},{4,3},{5,4},{6,5},{7,6},{8,7},{9,8},{10,9... | collective-permute-start | bytes 98312 | tf_op jit(solution)/shard_map/ppermute | solution.py:18
  24.1 2.6 %copy-start.15 = (f32[8]{0:T(128)S(1)}, f32[8]{0:T(128)}, u32[]{:S(2)}) copy-start(f32[8]{0:T(128)} %param.12) | copy-start | bytes 100
  24.1 3.3 %copy-start.3 = (s32[16,16,128]{2,1,0:T(8,128)S(1)}, s32[16,16,128]{2,1,0:T(8,128)}, u32[]{:S(2)}) copy-start(s32[16,16,128]{2,1,0:T(8,128)} %param.10) | copy-start | bytes 393220
  24.2 3.3 %copy-start.5 = (s32[16,16,128]{2,1,0:T(8,128)S(1)}, s32[16,16,128]{2,1,0:T(8,128)}, u32[]{:S(2)}) copy-start(s32[16,16,128]{2,1,0:T(8,128)} %param.9) | copy-start | bytes 393220
  24.2 16.3 %copy-start = (f32[2,3,16,16,128]{4,3,2,1,0:T(8,128)S(1)}, f32[2,3,16,16,128]{4,3,2,1,0:T(8,128)}, u32[]{:S(2)}) copy-start(f32[2,3,16,16,128]{4,3,2,1,0:T(8,128)} %param.7) | copy-start | bytes 2359300
  27.4 11.0 %copy-start.16 = (f32[2]{0:T(128)S(1)}, f32[2]{0:T(128)}, u32[]{:S(2)}) copy-start(f32[2]{0:T(128)} %param.13) | copy-start | bytes 28
  41.8 1.0 copy-start.2
  42.8 1.1 copy-start.1
  43.9 2.9 %copy-start.8 = (pred[16,16,128]{2,1,0:T(8,128)(4,1)S(1)}, pred[16,16,128]{2,1,0:T(8,128)(4,1)}, u32[]{:S(2)}) copy-start(pred[16,16,128]{2,1,0:T(8,128)(4,1)} %get-tuple-element.7) | copy-start | bytes 98308
  43.9 2.9 %copy-start.9 = (pred[16,16,128]{2,1,0:T(8,128)(4,1)S(1)}, pred[16,16,128]{2,1,0:T(8,128)(4,1)}, u32[]{:S(2)}) copy-start(pred[16,16,128]{2,1,0:T(8,128)(4,1)} %get-tuple-element.8) | copy-start | bytes 98308
  43.9 2.9 %copy-start.10 = (pred[16,16,128]{2,1,0:T(8,128)(4,1)S(1)}, pred[16,16,128]{2,1,0:T(8,128)(4,1)}, u32[]{:S(2)}) copy-start(pred[16,16,128]{2,1,0:T(8,128)(4,1)} %get-tuple-element.9) | copy-start | bytes 98308
  43.9 2.9 %copy-start.11 = (pred[16,16,128]{2,1,0:T(8,128)(4,1)S(1)}, pred[16,16,128]{2,1,0:T(8,128)(4,1)}, u32[]{:S(2)}) copy-start(pred[16,16,128]{2,1,0:T(8,128)(4,1)} %get-tuple-element.10) | copy-start | bytes 98308
  43.9 2.9 %copy-start.12 = (pred[16,16,128]{2,1,0:T(8,128)(4,1)S(1)}, pred[16,16,128]{2,1,0:T(8,128)(4,1)}, u32[]{:S(2)}) copy-start(pred[16,16,128]{2,1,0:T(8,128)(4,1)} %get-tuple-element.11) | copy-start | bytes 98308
  44.0 2.9 %copy-start.13 = (pred[16,16,128]{2,1,0:T(8,128)(4,1)S(1)}, pred[16,16,128]{2,1,0:T(8,128)(4,1)}, u32[]{:S(2)}) copy-start(pred[16,16,128]{2,1,0:T(8,128)(4,1)} %get-tuple-element.12) | copy-start | bytes 98308
  44.3 2.6 %copy-start.6 = (pred[16,16,128]{2,1,0:T(8,128)(4,1)S(1)}, pred[16,16,128]{2,1,0:T(8,128)(4,1)}, u32[]{:S(2)}) copy-start(pred[16,16,128]{2,1,0:T(8,128)(4,1)} %get-tuple-element.5) | copy-start | bytes 98308
  44.3 2.6 %copy-start.7 = (pred[16,16,128]{2,1,0:T(8,128)(4,1)S(1)}, pred[16,16,128]{2,1,0:T(8,128)(4,1)}, u32[]{:S(2)}) copy-start(pred[16,16,128]{2,1,0:T(8,128)(4,1)} %get-tuple-element.6) | copy-start | bytes 98308
  44.9 20.6 %collective-permute-start.2 = (f32[2,2,16,1,128]{4,2,3,1,0:T(8,128)}, f32[2,2,16,1,128]{4,2,3,1,0:T(8,128)}, u32[]{:S(2)}, u32[]{:S(2)}) collective-permute-start(f32[2,2,16,1,128]{4,2,3,1,0:T(8,128)} %slice.532), channel_id=1, source_target_pairs={{0,1},{1,2},{2,3},{3,4},{4,5},{5,6},{6,7},{7,8},{8,9},{9,10},{10,1... | collective-permute-start | bytes 98312 | tf_op jit(solution)/shard_map/ppermute | solution.py:18
  59.2 1.0 copy-start.4
  60.4 6.1 %collective-permute-start.3 = (f32[2,2,1,16,128]{4,2,3,0,1:T(1,128)S(1)}, f32[2,2,1,16,128]{4,2,3,0,1:T(1,128)S(1)}, u32[]{:S(2)}, u32[]{:S(2)}) collective-permute-start(f32[2,2,1,16,128]{4,2,3,0,1:T(1,128)S(1)} %copy.201), channel_id=1, source_target_pairs={{0,96},{96,192},{192,288},{288,384},{384,480},{480,576},{576,672},... | collective-permute-start | bytes 98312 | tf_op jit(solution)/shard_map/ppermute | solution.py:18
  67.2 14.3 %collective-permute-start.4 = (f32[2,2,16,1,128]{4,2,3,0,1:T(8,128)S(1)}, f32[2,2,16,1,128]{4,2,3,0,1:T(8,128)S(1)}, u32[]{:S(2)}, u32[]{:S(2)}) collective-permute-start(f32[2,2,16,1,128]{4,2,3,0,1:T(8,128)S(1)} %copy.204), channel_id=1, source_target_pairs={{0,95},{1,0},{2,1},{3,2},{4,3},{5,4},{6,5},{7,6},{8,7},{9,8},{10,9... | collective-permute-start | bytes 98312 | tf_op jit(solution)/shard_map/ppermute | solution.py:18
  79.1 7.9 %collective-permute-start.5 = (f32[2,2,1,16,128]{4,2,3,1,0:T(1,128)S(1)}, f32[2,2,1,16,128]{4,2,3,1,0:T(1,128)S(1)}, u32[]{:S(2)}, u32[]{:S(2)}) collective-permute-start(f32[2,2,1,16,128]{4,2,3,1,0:T(1,128)S(1)} %slice.685), channel_id=1, source_target_pairs={{0,672},{96,0},{192,96},{288,192},{384,288},{480,384},{576,480},{6... | collective-permute-start | bytes 98312 | tf_op jit(solution)/shard_map/ppermute | solution.py:18
  88.0 3.9 %collective-permute-start.7 = (f32[2,2,1,16,128]{4,2,3,0,1:T(1,128)S(1)}, f32[2,2,1,16,128]{4,2,3,0,1:T(1,128)S(1)}, u32[]{:S(2)}, u32[]{:S(2)}) collective-permute-start(f32[2,2,1,16,128]{4,2,3,0,1:T(1,128)S(1)} %copy.212), channel_id=1, source_target_pairs={{0,96},{96,192},{192,288},{288,384},{384,480},{480,576},{576,672},... | collective-permute-start | bytes 98312 | tf_op jit(solution)/shard_map/ppermute | solution.py:18
  90.0 12.8 %collective-permute-start.6 = (f32[2,2,16,1,128]{4,2,3,1,0:T(8,128)S(1)}, f32[2,2,16,1,128]{4,2,3,1,0:T(8,128)S(1)}, u32[]{:S(2)}, u32[]{:S(2)}) collective-permute-start(f32[2,2,16,1,128]{4,2,3,1,0:T(8,128)S(1)} %slice.566), channel_id=1, source_target_pairs={{0,1},{1,2},{2,3},{3,4},{4,5},{5,6},{6,7},{7,8},{8,9},{9,10},{10,1... | collective-permute-start | bytes 98312 | tf_op jit(solution)/shard_map/ppermute | solution.py:18
  103.6 5.6 %collective-permute-start.8 = (f32[2,2,16,1,128]{4,2,3,0,1:T(8,128)S(1)}, f32[2,2,16,1,128]{4,2,3,0,1:T(8,128)S(1)}, u32[]{:S(2)}, u32[]{:S(2)}) collective-permute-start(f32[2,2,16,1,128]{4,2,3,0,1:T(8,128)S(1)} %copy.215), channel_id=1, source_target_pairs={{0,95},{1,0},{2,1},{3,2},{4,3},{5,4},{6,5},{7,6},{8,7},{9,8},{10,9... | collective-permute-start | bytes 98312 | tf_op jit(solution)/shard_map/ppermute | solution.py:18
  105.6 7.0 %collective-permute-start.9 = (f32[2,2,1,16,128]{4,2,3,1,0:T(1,128)S(1)}, f32[2,2,1,16,128]{4,2,3,1,0:T(1,128)S(1)}, u32[]{:S(2)}, u32[]{:S(2)}) collective-permute-start(f32[2,2,1,16,128]{4,2,3,1,0:T(1,128)S(1)} %slice.715), channel_id=1, source_target_pairs={{0,672},{96,0},{192,96},{288,192},{384,288},{480,384},{576,480},{6... | collective-permute-start | bytes 98312 | tf_op jit(solution)/shard_map/ppermute | solution.py:18
  113.8 5.3 %collective-permute-start.11 = (f32[2,2,1,16,128]{4,2,3,0,1:T(1,128)S(1)}, f32[2,2,1,16,128]{4,2,3,0,1:T(1,128)S(1)}, u32[]{:S(2)}, u32[]{:S(2)}) collective-permute-start(f32[2,2,1,16,128]{4,2,3,0,1:T(1,128)S(1)} %copy.223), channel_id=1, source_target_pairs={{0,96},{96,192},{192,288},{288,384},{384,480},{480,576},{576,672},... | collective-permute-start | bytes 98312 | tf_op jit(solution)/shard_map/ppermute | solution.py:18
  115.8 12.8 %collective-permute-start.10 = (f32[2,2,16,1,128]{4,2,3,1,0:T(8,128)S(1)}, f32[2,2,16,1,128]{4,2,3,1,0:T(8,128)S(1)}, u32[]{:S(2)}, u32[]{:S(2)}) collective-permute-start(f32[2,2,16,1,128]{4,2,3,1,0:T(8,128)S(1)} %slice.600), channel_id=1, source_target_pairs={{0,1},{1,2},{2,3},{3,4},{4,5},{5,6},{6,7},{7,8},{8,9},{9,10},{10,1... | collective-permute-start | bytes 98312 | tf_op jit(solution)/shard_map/ppermute | solution.py:18
  129.4 5.6 %collective-permute-start.12 = (f32[2,2,16,1,128]{4,2,3,1,0:T(8,128)S(1)}, f32[2,2,16,1,128]{4,2,3,1,0:T(8,128)S(1)}, u32[]{:S(2)}, u32[]{:S(2)}) collective-permute-start(f32[2,2,16,1,128]{4,2,3,1,0:T(8,128)S(1)} %slice.617), channel_id=1, source_target_pairs={{0,95},{1,0},{2,1},{3,2},{4,3},{5,4},{6,5},{7,6},{8,7},{9,8},{10,9... | collective-permute-start | bytes 98312 | tf_op jit(solution)/shard_map/ppermute | solution.py:18
  131.5 7.0 %collective-permute-start.13 = (f32[2,2,1,16,128]{4,2,3,1,0:T(1,128)S(1)}, f32[2,2,1,16,128]{4,2,3,1,0:T(1,128)S(1)}, u32[]{:S(2)}, u32[]{:S(2)}) collective-permute-start(f32[2,2,1,16,128]{4,2,3,1,0:T(1,128)S(1)} %slice.745), channel_id=1, source_target_pairs={{0,672},{96,0},{192,96},{288,192},{384,288},{480,384},{576,480},{6... | collective-permute-start | bytes 98312 | tf_op jit(solution)/shard_map/ppermute | solution.py:18
  139.6 12.8 %collective-permute-start.14 = (f32[2,2,16,1,128]{4,2,3,1,0:T(8,128)S(1)}, f32[2,2,16,1,128]{4,2,3,1,0:T(8,128)S(1)}, u32[]{:S(2)}, u32[]{:S(2)}) collective-permute-start(f32[2,2,16,1,128]{4,2,3,1,0:T(8,128)S(1)} %slice.634), channel_id=1, source_target_pairs={{0,1},{1,2},{2,3},{3,4},{4,5},{5,6},{6,7},{7,8},{8,9},{9,10},{10,1... | collective-permute-start | bytes 98312 | tf_op jit(solution)/shard_map/ppermute | solution.py:18
  144.2 8.2 %collective-permute-start.15 = (f32[2,2,1,16,128]{4,2,3,0,1:T(1,128)S(1)}, f32[2,2,1,16,128]{4,2,3,0,1:T(1,128)S(1)}, u32[]{:S(2)}, u32[]{:S(2)}) collective-permute-start(f32[2,2,1,16,128]{4,2,3,0,1:T(1,128)S(1)} %copy.233), channel_id=1, source_target_pairs={{0,96},{96,192},{192,288},{288,384},{384,480},{480,576},{576,672},... | collective-permute-start | bytes 98312 | tf_op jit(solution)/shard_map/ppermute | solution.py:18
where the time goes:
time: 156 us; the launch traced here: 155 us
  starting transfers between devices  68.3 us (44%)
  waiting for transfers between devices  38.5 us (25%)
  other arithmetic  29.2 us (19%)
  local copies, waits for them, and re-layouts  13.8 us (9%)
  between operations  4.65 us (3%)
    ppermute x16, starting transfers between devices, shifted(): return lax.ppermute(value, axis, pairs)  68.3 us
    ppermute x16, waiting for transfers between devices, shifted(): return lax.ppermute(value, axis, pairs)  38.5 us
    div x1, other arithmetic, coefficients(): scale = (1.0 - half_loss) / (1.0 + half_loss)  11 us
    div x1, other arithmetic, coefficients(): drive = TIME_STEP / (permittivity_cells * (1.0 + half_loss))  10.8 us
    unnamed x47, local copies, waits for them, and re-layouts  4.73 us
  transfers between devices with their start and end apart: 16, of which 7 were waited for; matrix products, arithmetic and copies ran while one was open for 20% of the time, Pallas kernels for 0%

commit v1 on v0

v1 whole, which is shorter than its diff:
```python
import jax
import jax.numpy as jnp
from jax import lax
from jax.experimental import pallas as pl
from jax.experimental.pallas import tpu as pltpu
from jax.sharding import PartitionSpec as P

ABSORB = 10
TIME_STEP = 0.55
ABSORB_PEAK = 1.5

OX, OY = 4, 8
XW, YW = 24, 32
LANES = 128
F32 = jnp.float32

TO_NEXT = (
    ("E", (0, 1, 2), (-3, -2, -1, 16, 17, 18, 19), 15),
    ("H", (0, 1, 2), (-3, -2, -1, 16, 17, 18), 15),
    ("H", (0, 1, 2), (-2, -1, 15, 16, 17, 18), 14),
    ("E", (0, 1, 2), (-1, 0, 15, 16, 17, 18), 14),
    ("H", (0, 2), (0, 14, 15, 16, 17), 13),
)
TO_PREV = (
    ("E", (0, 1, 2), (-4, -3, -2, -1, 16, 17, 18), 0),
    ("H", (0, 1, 2), (-4, -3, -2, -1, 15, 16, 17), 0),
    ("E", (0, 2), (-3, -2, -1, 0, 15, 16), 1),
    ("H", (0, 1, 2), (-3, -2, -1, 0, 14, 15), 1),
)
CELLS_NEXT = tuple((x, 15) for x in (-3, -2, -1, 16, 17, 18)) + tuple((x, 14) for x in (-1, 16, 17))
CELLS_PREV = tuple((x, 0) for x in (-3, -2, -1, 16, 17)) + tuple((x, 1) for x in (-2, -1))

X_TO_NEXT = (
    ("E", (0, 1, 2), (13,), 15),
    ("H", (0,), (13,), 15),
    ("E", (0, 1, 2), (12, 13), 0),
    ("H", (0, 1, 2), (12,), 0),
    ("H", (0,), (13,), 0),
    ("E", (0, 2), (13,), 1),
    ("H", (0,), (13,), 1),
    ("E", (0, 1, 2), (12,), 15),
    ("H", (1, 2), (12,), 15),
    ("E", (0, 1, 2), (13,), 14),
    ("H", (0,), (13,), 14),
)
X_TO_PREV = (
    ("E", (0, 1, 2), (2, 3), 15),
    ("H", (0, 1, 2), (2,), 15),
    ("H", (0, 1, 2), (2,), 14),
    ("E", (0, 1, 2), (2,), 14),
    ("E", (0, 1, 2), (2,), 0),
    ("H", (0, 1, 2), (2,), 0),
)
X_CELLS_NEXT = ((13, 15), (13, 0), (12, 15), (13, 14))
X_CELLS_PREV = ((2, 15), (2, 0))


def entries(face):
    return [(name, c, x, row) for name, comps, columns, row in face for c in comps for x in columns]


LIST_NEXT, LIST_PREV = entries(TO_NEXT), entries(TO_PREV)
HALF = max(len(LIST_NEXT), len(LIST_PREV))
CORNER_ROWS = -(-(2 * HALF + 2 * max(len(CELLS_NEXT), len(CELLS_PREV))) // 8) * 8

X_LIST_NEXT, X_LIST_PREV = entries(X_TO_NEXT), entries(X_TO_PREV)
X_HALF = max(len(X_LIST_NEXT), len(X_LIST_PREV))
X_SLABS = 32 + -(-(2 * X_HALF + 2 * len(X_CELLS_NEXT)) // 16)


def ghost_row(row):
    return row - 16 if row > 8 else row + 16


def lanes():
    return lax.broadcasted_iota(jnp.int32, (8, LANES), 1)


def ahead(v):
    return jnp.where(lanes() < LANES - 1, pltpu.roll(v, LANES - 1, 1), 0.0)


def behind(v):
    return jnp.where(lanes() > 0, pltpu.roll(v, 1, 1), 0.0)


def row_mask(start, low, high):
    y = lax.broadcasted_iota(jnp.int32, (8, LANES), 0) + (start - OY)
    return (y >= low) & (y < high)


def half_step(field, other, keep, gain, xlow, xhigh, windows, sign):
    along_z = ahead if sign == 1 else behind
    for X in range(xlow + OX, xhigh + OX):
        for start, low, high in windows:
            s, n = pl.ds(start, 8), pl.ds(start + sign, 8)
            whole = low <= start - OY and high >= start - OY + 8
            d, q = keep[X, s, :], gain[X, s, :]
            for p in range(2):
                fx, fy, fz = (other[p, c, X, s, :] for c in range(3))
                y_x, y_z = other[p, 0, X, n, :], other[p, 2, X, n, :]
                x_y, x_z = other[p, 1, X + sign, s, :], other[p, 2, X + sign, s, :]
                curl = (
                    (y_z - fz) - (along_z(fy) - fy),
                    (along_z(fx) - fx) - (x_z - fz),
                    (x_y - fy) - (y_x - fx),
                )
                for c in range(3):
                    old = field[p, c, X, s, :]
                    new = d * old - q * curl[c]
                    field[p, c, X, s, :] = new if whole else jnp.where(row_mask(start, low, high), new, old)


def half_h(E, H, decay, push, xlow, xhigh, windows):
    half_step(H, E, decay, push, xlow, xhigh, windows, 1)


def half_e(E, H, scale, drive, xlow, xhigh, windows):
    half_step(E, H, scale, drive, xlow, xhigh, windows, -1)


def own(low, high):
    return ((8, low, high), (16, low, high))


SIGMA, X_TURN, Y_TURN = 8, 16, 18


def coefficients(table, material, mask):
    eps = jnp.broadcast_to(table[0:1, :], material.shape)
    sigma = jnp.broadcast_to(table[SIGMA : SIGMA + 1, :], material.shape)
    for m in range(1, 8):
        chosen = material == float(m)
        eps = jnp.where(chosen, table[m : m + 1, :], eps)
        sigma = jnp.where(chosen, table[SIGMA + m : SIGMA + m + 1, :], sigma)
    k = lax.broadcasted_iota(jnp.int32, (1, LANES), 1).astype(F32)
    reach = jnp.maximum(jnp.maximum(ABSORB - k, k - (LANES - 1 - ABSORB)), 0.0) / ABSORB
    magnetic_loss = mask * (ABSORB_PEAK * (reach * reach * reach))
    half = (sigma + magnetic_loss) * (TIME_STEP / 2.0) / eps
    below = 1.0 / (1.0 + half)
    half_m = magnetic_loss * (TIME_STEP / 2.0)
    below_m = 1.0 / (1.0 + half_m)
    return (1.0 - half) * below, (TIME_STEP / eps) * below, (1.0 - half_m) * below_m, TIME_STEP * below_m


def set_coefficients(table, state, X, s, material, mask):
    for ref, value in zip(state, coefficients(table, material, mask)):
        ref[X, s, :] = value


def edge_turn(axis, angle):
    index = lax.axis_index(axis)
    return jnp.where(index == 0, -angle, jnp.where(index == lax.axis_size(axis) - 1, angle, 0.0))


def is_odd(axis):
    return lax.rem(lax.axis_index(axis), 2) == 1


def either(odd, make, a, b):
    pl.when(odd)(lambda: make(b, a))
    pl.when(jnp.logical_not(odd))(lambda: make(a, b))


def turned(table, row, re, im):
    cosine, sine = table[row : row + 1, :], table[row + 1 : row + 2, :]
    return re * cosine - im * sine, re * sine + im * cosine


def pack_y(buf, E, H, mat, mask, rows, extra):
    for x in range(16):
        X = x + OX
        for p in range(2):
            for c in range(3):
                at = 4 * (3 * p + c)
                buf[x, at : at + 2, :] = E[p, c, X, rows : rows + 2, :]
                buf[x, at + 2 : at + 4, :] = H[p, c, X, rows : rows + 2, :]
        if extra is not None:
            for p in range(2):
                for i, c in enumerate((0, 2)):
                    at = 24 + 2 * p + i
                    buf[x, at : at + 1, :] = H[p, c, X, extra : extra + 1, :]
        buf[x, 28:30, :] = mat[X, rows : rows + 2, :]
        buf[x, 30:32, :] = mask[X, rows : rows + 2, :]


def pack_x(buf, E, H, mat, mask, first, extra, items, cells):
    columns, rows = pl.ds(first + OX, 2), pl.ds(OY, 16)
    for p in range(2):
        for c in range(3):
            at = 2 * (3 * p + c)
            buf[at : at + 2] = E[p, c, columns, rows, :]
            buf[12 + at : 14 + at] = H[p, c, columns, rows, :]
    if extra is not None:
        for p in range(2):
            for i, c in enumerate((1, 2)):
                buf[24 + 2 * p + i] = H[p, c, extra + OX, rows, :]
    buf[28:30] = mat[columns, rows, :]
    buf[30:32] = mask[columns, rows, :]

    def put(row, value):
        buf[32 + row // 16, row % 16 : row % 16 + 1, :] = value

    pack_rows(put, E, H, mat, mask, items, cells, X_HALF)


def pack_rows(put, E, H, mat, mask, items, cells, half):
    for i, (name, c, x, row) in enumerate(items):
        field = E if name == "E" else H
        for p in range(2):
            put(p * half + i, field[p, c, x + OX, row + OY : row + OY + 1, :])
    for i, (x, row) in enumerate(cells):
        put(2 * half + 2 * i, mat[x + OX, row + OY : row + OY + 1, :])
        put(2 * half + 2 * i + 1, mask[x + OX, row + OY : row + OY + 1, :])


def unpack_rows(get, E, H, mat, mask, items, cells, half, turn, place):
    for i, (name, c, x, row) in enumerate(items):
        field = E if name == "E" else H
        X, R = place(x, row)
        re, im = turn(get(i), get(half + i))
        field[0, c, X, R : R + 1, :] = re
        field[1, c, X, R : R + 1, :] = im
    for i, (x, row) in enumerate(cells):
        X, R = place(x, row)
        mat[X, R : R + 1, :] = get(2 * half + 2 * i)
        mask[X, R : R + 1, :] = get(2 * half + 2 * i + 1)


def first_kernel(
    e_in, h_in, mat_in, mask_in, eps_in, sigma_in, phase_in,
    E, H, scale, drive, decay, push, mat, mask, table, xa, xb, ya, yb,
    raw_mat, raw_mask, eps, sigma, phase, sems,
):
    state = (scale, drive, decay, push)
    inside = (slice(None), slice(None), pl.ds(OX, 16), pl.ds(OY, 16), slice(None))
    pairs = [
        (eps_in, eps),
        (sigma_in, sigma),
        (phase_in, phase),
        (mat_in, raw_mat),
        (mask_in, raw_mask),
        (e_in, E.at[inside]),
        (h_in, H.at[inside]),
    ]
    copies = [pltpu.make_async_copy(a, b, sems.at[i]) for i, (a, b) in enumerate(pairs)]
    for copy in copies:
        copy.start()
    for copy in copies[:3]:
        copy.wait()
    for m in range(8):
        table[m : m + 1, :] = jnp.full((1, LANES), eps[m], F32)
        table[SIGMA + m : SIGMA + m + 1, :] = jnp.full((1, LANES), sigma[m], F32)
    for axis, row, i in (("gx", X_TURN, 0), ("gy", Y_TURN, 1)):
        angle = jnp.full((1, LANES), edge_turn(axis, phase[i]), F32)
        table[row : row + 1, :] = jnp.cos(angle)
        table[row + 1 : row + 2, :] = jnp.sin(angle)
    copies[3].wait()
    copies[4].wait()
    for x in range(16):
        for start in (0, 8):
            s, t = pl.ds(start, 8), pl.ds(start + OY, 8)
            m, k = raw_mat[x, s, :].astype(F32), raw_mask[x, s, :].astype(F32)
            mat[x + OX, t, :] = m
            mask[x + OX, t, :] = k
            set_coefficients(table, state, x + OX, t, m, k)
    copies[5].wait()
    copies[6].wait()

    half_h(E, H, decay, push, 0, 15, own(0, 15))
    half_e(E, H, scale, drive, 1, 15, own(1, 15))
    half_h(E, H, decay, push, 1, 14, own(1, 14))

    def x_faces(to_next, to_prev):
        pack_x(to_next, E, H, mat, mask, 14, 13, X_LIST_NEXT, X_CELLS_NEXT)
        pack_x(to_prev, E, H, mat, mask, 0, None, X_LIST_PREV, X_CELLS_PREV)

    def y_faces(to_next, to_prev):
        pack_y(to_next, E, H, mat, mask, OY + 14, OY + 13)
        pack_y(to_prev, E, H, mat, mask, OY, None)

    either(is_odd("gx"), x_faces, xa, xb)
    either(is_odd("gy"), y_faces, ya, yb)


def second_kernel(
    xb, xa, table, e_io, h_io, s_io, d_io, c_io, p_io, m_io, k_io,
    E, H, scale, drive, decay, push, mat, mask, ya, yb,
):
    state = (scale, drive, decay, push)
    rows = pl.ds(OY, 16)

    def place(buf, first, extra, items, cells, shift, edge):
        def turn(re, im):
            return turned(table, X_TURN, re, im) if edge else (re, im)

        for field, base in ((E, 0), (H, 12)):
            for c in range(3):
                at = base + 2 * c
                for j in range(2):
                    re, im = turn(buf[at + j], buf[at + 6 + j])
                    field[0, c, first + OX + j, rows, :] = re
                    field[1, c, first + OX + j, rows, :] = im
        if extra is not None:
            for i, c in enumerate((1, 2)):
                re, im = turn(buf[24 + i], buf[26 + i])
                H[0, c, extra + OX, rows, :] = re
                H[1, c, extra + OX, rows, :] = im
        for j in range(2):
            X = first + OX + j
            for start in (0, 8):
                s, t = pl.ds(start, 8), pl.ds(start + OY, 8)
                m, k = buf[28 + j, s, :], buf[30 + j, s, :]
                mat[X, t, :] = m
                mask[X, t, :] = k
                set_coefficients(table, state, X, t, m, k)

        def get(row):
            return buf[32 + row // 16, row % 16 : row % 16 + 1, :]

        unpack_rows(
            get, E, H, mat, mask, items, cells, X_HALF, turn, lambda x, row: (x + shift + OX, row + OY)
        )

    def ghosts(above, below, odd):
        place(below, -2, -3, X_LIST_NEXT, X_CELLS_NEXT, -16, not odd)
        place(above, 16, None, X_LIST_PREV, X_CELLS_PREV, 16, odd)

    gx_odd = is_odd("gx")
    pl.when(gx_odd)(lambda: ghosts(xb, xa, True))
    pl.when(jnp.logical_not(gx_odd))(lambda: ghosts(xa, xb, False))

    for X in (0, 1, 22):
        for start in (8, 16):
            s = pl.ds(start, 8)
            set_coefficients(table, state, X, s, mat[X, s, :], mask[X, s, :])

    half_h(E, H, decay, push, -1, 0, own(0, 15))
    half_h(E, H, decay, push, 15, 16, own(0, 15))
    half_e(E, H, scale, drive, -1, 1, own(1, 15))
    half_e(E, H, scale, drive, 15, 17, own(1, 15))
    half_h(E, H, decay, push, -2, 1, own(1, 14))
    half_h(E, H, decay, push, 14, 17, own(1, 14))

    def pack(to_next, to_prev):
        for buf, items, cells in ((to_next, LIST_NEXT, CELLS_NEXT), (to_prev, LIST_PREV, CELLS_PREV)):

            def put(row, value, buf=buf):
                buf[row : row + 1, :] = value

            pack_rows(put, E, H, mat, mask, items, cells, HALF)

    either(is_odd("gy"), pack, ya, yb)


def third_kernel(
    e_io, h_io, s_io, d_io, c_io, p_io,
    E, H, scale, drive, decay, push,
):
    half_e(E, H, scale, drive, -2, 18, own(2, 14))
    half_h(E, H, decay, push, -2, 17, own(2, 13))
    half_e(E, H, scale, drive, -1, 17, own(3, 13))
    half_h(E, H, decay, push, -1, 16, own(3, 12))
    half_e(E, H, scale, drive, 0, 16, own(4, 12))


def last_kernel(
    yb, ya, zb, za, table, e_io, h_io, s_io, d_io, c_io, p_io,
    e_out, h_out, E, H, scale, drive, decay, push,
    mat, mask, sems,
):
    state = (scale, drive, decay, push)

    def unpack_y(buf, rows, extra, edge):
        def turn(re, im):
            return turned(table, Y_TURN, re, im) if edge else (re, im)

        for x in range(16):
            X = x + OX
            for c in range(3):
                for f, field in enumerate((E, H)):
                    re, im = (buf[x, 4 * (3 * p + c) + 2 * f : 4 * (3 * p + c) + 2 * f + 2, :] for p in range(2))
                    re, im = turn(re, im)
                    field[0, c, X, rows : rows + 2, :] = re
                    field[1, c, X, rows : rows + 2, :] = im
            if extra is not None:
                for i, c in enumerate((0, 2)):
                    re, im = turn(buf[x, 24 + i : 25 + i, :], buf[x, 26 + i : 27 + i, :])
                    H[0, c, X, extra : extra + 1, :] = re
                    H[1, c, X, extra : extra + 1, :] = im
            mat[X, rows : rows + 2, :] = buf[x, 28:30, :]
            mask[X, rows : rows + 2, :] = buf[x, 30:32, :]

    def ghosts(above, below, above_far, below_far, odd):
        unpack_y(below, OY - 2, OY - 3, not odd)
        unpack_y(above, OY + 16, None, odd)
        for buf, items, cells, edge in (
            (below_far, LIST_NEXT, CELLS_NEXT, not odd),
            (above_far, LIST_PREV, CELLS_PREV, odd),
        ):

            def turn(re, im, edge=edge):
                return turned(table, Y_TURN, re, im) if edge else (re, im)

            unpack_rows(
                lambda row, buf=buf: buf[row : row + 1, :],
                E, H, mat, mask, items, cells, HALF, turn,
                lambda x, row: (x + OX, ghost_row(row) + OY),
            )

    gy_odd = is_odd("gy")
    pl.when(gy_odd)(lambda: ghosts(yb, ya, zb, za, True))
    pl.when(jnp.logical_not(gy_odd))(lambda: ghosts(ya, yb, za, zb, False))

    for X in range(1, XW - 1):
        for start in (0, 24):
            s = pl.ds(start, 8)
            set_coefficients(table, state, X, s, mat[X, s, :], mask[X, s, :])

    def sides(low, low_end, high, high_end):
        return ((4, low, low_end), (20, high, high_end))

    half_h(E, H, decay, push, -4, 19, sides(-1, 0, 15, 16))
    half_e(E, H, scale, drive, -3, 19, sides(-1, 1, 15, 17))
    half_h(E, H, decay, push, -3, 18, sides(-2, 1, 14, 17))
    half_e(E, H, scale, drive, -2, 18, sides(-2, 2, 14, 18))
    half_h(E, H, decay, push, -2, 17, sides(-2, 2, 13, 17))
    half_e(E, H, scale, drive, -1, 17, sides(-1, 3, 13, 17))
    half_h(E, H, decay, push, -1, 16, sides(-1, 3, 12, 16))
    inside = (slice(None), slice(None), pl.ds(OX, 16), pl.ds(OY, 16), slice(None))
    copy_h = pltpu.make_async_copy(H.at[inside], h_out, sems.at[0])
    copy_h.start()
    half_e(E, H, scale, drive, 0, 16, sides(0, 4, 12, 16))
    copy_e = pltpu.make_async_copy(E.at[inside], e_out, sems.at[1])
    copy_e.start()
    copy_h.wait()
    copy_e.wait()


VMEM = pl.BlockSpec(memory_space=pltpu.VMEM)
HBM = pl.BlockSpec(memory_space=pltpu.HBM)
FIELD = jax.ShapeDtypeStruct((2, 3, XW, YW, LANES), F32)
CELL = jax.ShapeDtypeStruct((XW, YW, LANES), F32)
TABLE = jax.ShapeDtypeStruct((24, LANES), F32)
X_FACE = jax.ShapeDtypeStruct((X_SLABS, 16, LANES), F32)
Y_FACE = jax.ShapeDtypeStruct((16, 32, LANES), F32)
FAR_FACE = jax.ShapeDtypeStruct((CORNER_ROWS, LANES), F32)
PARAMS = pltpu.CompilerParams(vmem_limit_bytes=32 * 1024 * 1024)


def swapped(value, axis, odd):
    count = lax.axis_size(axis)
    pairs = []
    for low in range(odd, count, 2):
        high = (low + 1) % count
        pairs += [(low, high), (high, low)]
    return lax.ppermute(value, axis, pairs)


def per_device(electric, magnetic, material, absorber_mask, permittivity, conductivity, bloch_phase):
    out = pl.pallas_call(
        first_kernel,
        out_shape=(FIELD, FIELD) + (CELL,) * 6 + (TABLE, X_FACE, X_FACE, Y_FACE, Y_FACE),
        in_specs=[HBM] * 7,
        out_specs=(VMEM,) * 13,
        scratch_shapes=[
            pltpu.VMEM((16, 16, LANES), jnp.int32),
            pltpu.VMEM((16, 16, LANES), jnp.int32),
            pltpu.SMEM((8,), F32),
            pltpu.SMEM((8,), F32),
            pltpu.SMEM((2,), F32),
            pltpu.SemaphoreType.DMA((7,)),
        ],
        compiler_params=PARAMS,
        name="first",
    )(*(pltpu.with_memory_space_constraint(v, pltpu.HBM) for v in (electric, magnetic, material, absorber_mask, permittivity, conductivity, bloch_phase)))
    state, table, (xa, xb, ya, yb) = out[:8], out[8], out[9:]
    xb = swapped(xb, "gx", 1)
    yb = swapped(yb, "gy", 1)
    xa = swapped(xa, "gx", 0)
    ya = swapped(ya, "gy", 0)
    out = pl.pallas_call(
        second_kernel,
        out_shape=(FIELD, FIELD) + (CELL,) * 6 + (FAR_FACE, FAR_FACE),
        in_specs=[VMEM] * 11,
        out_specs=(VMEM,) * 10,
        input_output_aliases={3 + i: i for i in range(8)},
        compiler_params=PARAMS,
        name="second",
    )(xb, xa, table, *state)
    state, (za, zb) = out[:6], out[8:]
    zb = swapped(zb, "gy", 1)
    za = swapped(za, "gy", 0)
    state = pl.pallas_call(
        third_kernel,
        out_shape=(FIELD, FIELD) + (CELL,) * 4,
        in_specs=[VMEM] * 6,
        out_specs=(VMEM,) * 6,
        input_output_aliases={i: i for i in range(6)},
        compiler_params=PARAMS,
        name="third",
    )(*state)
    out = pl.pallas_call(
        last_kernel,
        out_shape=(
            jax.ShapeDtypeStruct(electric.shape, F32),
            jax.ShapeDtypeStruct(magnetic.shape, F32),
            FIELD,
            FIELD,
        )
        + (CELL,) * 4,
        in_specs=[VMEM] * 11,
        out_specs=(HBM, HBM) + (VMEM,) * 6,
        input_output_aliases={5 + i: 2 + i for i in range(6)},
        scratch_shapes=[
            pltpu.VMEM(CELL.shape, F32),
            pltpu.VMEM(CELL.shape, F32),
            pltpu.SemaphoreType.DMA((2,)),
        ],
        compiler_params=PARAMS,
        name="last",
    )(yb, ya, zb, za, table, *state)
    return out[0], out[1]


def solution(mesh):
    field = P(None, None, "gx", "gy", None)
    cell = P("gx", "gy", None)
    return jax.shard_map(
        per_device,
        mesh=mesh,
        in_specs=(field, field, cell, cell, P(), P(), P()),
        out_specs=(field, field),
        check_vma=False,
    )
```

time: 156 us -> 64.3 us (0.41)
  the two profiles are of different devices: /device:TPU:25 before, /device:TPU:2 now
where the time goes in v1:
time: 64.3 us; the launch traced here: 64 us
  starting transfers between devices  52.3 us (81%)
  Pallas kernels  10.5 us (16%)
  between operations  0.74 us (1%)
    ppermute x6, starting transfers between devices, swapped(): return lax.ppermute(value, axis, pairs)  52.3 us
    pallas_call x1, Pallas kernels, per_device(): pl.pallas_call(last_kernel, out_shape=(jax.ShapeDtypeStruct(electric.shap...  4.91 us
    pallas_call x1, Pallas kernels, per_device(): pl.pallas_call(first_kernel, out_shape=(FIELD, FIELD) + (CELL,) * 6 + (TA...  2.83 us
    pallas_call x1, Pallas kernels, per_device(): pl.pallas_call(third_kernel, out_shape=(FIELD, FIELD) + (CELL,) * 4, in_s...  2.17 us
  transfers between devices with their start and end apart: 6, of which 1 were waited for; matrix products, arithmetic and copies ran while one was open for 0% of the time, Pallas kernels for 4%

profile of v1, /device:TPU:2, one launch (start us, length us, event | category | flops | bytes accessed | tf_op | source)
XLA Modules:
  0.0 64.0 jit_solution(5309573729578744583)
XLA Ops:
  0.6 2.8 %first.1 = (f32[2,3,24,32,128]{4,3,2,1,0:T(8,128)S(1)}, f32[2,3,24,32,128]{4,3,2,1,0:T(8,128)S(1)}, f32[24,32,128]{2,1,0:T(8,128)S(1)}, f32[24,32,128]{2,1,0:T(8...) custom-call(f32[2,3,16,16,128]{4,3,2,1,0:T(8,128)} %e_in.1, ...), custom_call_target="tpu_custom_call" | custom-call | tf_op jit(solution)/shard_map/first/pallas_call | solution.py:461
  3.5 5.0 %collective-permute-start.2 = (f32[36,16,128]{2,1,0:T(8,128)S(1)}, f32[36,16,128]{2,1,0:T(8,128)S(1)}, u32[]{:S(2)}, u32[]{:S(2)}) collective-permute-start(f32[36,16,128]{2,1,0:T(8,128)S(1)} %get-tuple-element.33), channel_id=1, source_target_pairs={{96,192},{192,96},{288,384},{384,288},{480,576},{576,480},{672,0},... | collective-permute-start | bytes 884744 | tf_op jit(solution)/shard_map/ppermute | solution.py:457
  8.4 1.9 %collective-permute-start.3 = (f32[36,16,128]{2,1,0:T(8,128)S(1)}, f32[36,16,128]{2,1,0:T(8,128)S(1)}, u32[]{:S(2)}, u32[]{:S(2)}) collective-permute-start(f32[36,16,128]{2,1,0:T(8,128)S(1)} %get-tuple-element.34), channel_id=1, source_target_pairs={{0,96},{96,0},{192,288},{288,192},{384,480},{480,384},{576,672},{6... | collective-permute-start | bytes 884744 | tf_op jit(solution)/shard_map/ppermute | solution.py:457
  10.4 3.4 %collective-permute-start = (f32[16,32,128]{2,1,0:T(8,128)S(1)}, f32[16,32,128]{2,1,0:T(8,128)S(1)}, u32[]{:S(2)}, u32[]{:S(2)}) collective-permute-start(f32[16,32,128]{2,1,0:T(8,128)S(1)} %get-tuple-element.31), channel_id=1, source_target_pairs={{1,2},{2,1},{3,4},{4,3},{5,6},{6,5},{7,8},{8,7},{9,10},{10,9},{11,... | collective-permute-start | bytes 786440 | tf_op jit(solution)/shard_map/ppermute | solution.py:457
  13.8 18.8 %collective-permute-start.1 = (f32[16,32,128]{2,1,0:T(8,128)S(1)}, f32[16,32,128]{2,1,0:T(8,128)S(1)}, u32[]{:S(2)}, u32[]{:S(2)}) collective-permute-start(f32[16,32,128]{2,1,0:T(8,128)S(1)} %get-tuple-element.32), channel_id=1, source_target_pairs={{0,1},{1,0},{2,3},{3,2},{4,5},{5,4},{6,7},{7,6},{8,9},{9,8},{10,11... | collective-permute-start | bytes 786440 | tf_op jit(solution)/shard_map/ppermute | solution.py:457
  32.6 0.0 collective-permute-done.2.xb
  32.6 0.0 collective-permute-done.3.xa
  32.6 0.6 second.1
  33.2 1.9 %collective-permute-start.4 = (f32[192,128]{1,0:T(8,128)S(1)}, f32[192,128]{1,0:T(8,128)S(1)}, u32[]{:S(2)}, u32[]{:S(2)}) collective-permute-start(f32[192,128]{1,0:T(8,128)S(1)} %get-tuple-element.44), channel_id=1, source_target_pairs={{1,2},{2,1},{3,4},{4,3},{5,6},{6,5},{7,8},{8,7},{9,10},{10,9},{11,... | collective-permute-start | bytes 294920 | tf_op jit(solution)/shard_map/ppermute | solution.py:457
  35.1 21.3 %collective-permute-start.5 = (f32[192,128]{1,0:T(8,128)S(1)}, f32[192,128]{1,0:T(8,128)S(1)}, u32[]{:S(2)}, u32[]{:S(2)}) collective-permute-start(f32[192,128]{1,0:T(8,128)S(1)} %get-tuple-element.45), channel_id=1, source_target_pairs={{0,1},{1,0},{2,3},{3,2},{4,5},{5,4},{6,7},{7,6},{8,9},{9,8},{10,11... | collective-permute-start | bytes 294920 | tf_op jit(solution)/shard_map/ppermute | solution.py:457
  56.5 2.2 %third.1 = (f32[2,3,24,32,128]{4,3,2,1,0:T(8,128)S(1)}, f32[2,3,24,32,128]{4,3,2,1,0:T(8,128)S(1)}, f32[24,32,128]{2,1,0:T(8,128)S(1)}, f32[24,32,128]{2,1,0:T(8...) custom-call(f32[2,3,24,32,128]{4,3,2,1,0:T(8,128)S(1)} %get-tuple-el, ...), custom_call_target="tpu_custom_call", output_to_operand_aliasing={{0}: (0, {}), {1}: (1, {}), {2}: (2, {}), {3}: (3, {}), {4}... | custom-call | tf_op jit(solution)/shard_map/third/pallas_call | solution.py:494
  58.7 0.0 collective-permute-done.yb
  58.7 0.0 collective-permute-done.1.ya
  58.7 0.0 collective-permute-done.4.zb
  58.7 0.4 collective-permute-done.5.za
  59.1 4.9 %last.1 = (f32[2,3,16,16,128]{4,3,2,1,0:T(8,128)}, f32[2,3,16,16,128]{4,3,2,1,0:T(8,128)}, f32[2,3,24,32,128]{4,3,2,1,0:T(8,128)S(1)}, f32[2,3,24,32,128]{4,3,2,...) custom-call(f32[16,32,128]{2,1,0:T(8,128)S(1)} %collective-permute-d, ...), custom_call_target="tpu_custom_call", output_to_operand_aliasing={{2}: (5, {}), {3}: (6, {}), {4}: (7, {}), {5}: (8, {}), {6}... | custom-call | tf_op jit(solution)/shard_map/last/pallas_call | solution.py:503
Async XLA Ops:
  3.5 29.1 %collective-permute-start.2 = (f32[36,16,128]{2,1,0:T(8,128)S(1)}, f32[36,16,128]{2,1,0:T(8,128)S(1)}, u32[]{:S(2)}, u32[]{:S(2)}) collective-permute-start(f32[36,16,128]{2,1,0:T(8,128)S(1)} %get-tuple-element.33), channel_id=1, source_target_pairs={{96,192},{192,96},{288,384},{384,288},{480,576},{576,480},{672,0},... | collective-permute-start | bytes 884744 | tf_op jit(solution)/shard_map/ppermute | solution.py:457
  8.4 24.2 %collective-permute-start.3 = (f32[36,16,128]{2,1,0:T(8,128)S(1)}, f32[36,16,128]{2,1,0:T(8,128)S(1)}, u32[]{:S(2)}, u32[]{:S(2)}) collective-permute-start(f32[36,16,128]{2,1,0:T(8,128)S(1)} %get-tuple-element.34), channel_id=1, source_target_pairs={{0,96},{96,0},{192,288},{288,192},{384,480},{480,384},{576,672},{6... | collective-permute-start | bytes 884744 | tf_op jit(solution)/shard_map/ppermute | solution.py:457
  10.4 48.3 %collective-permute-start = (f32[16,32,128]{2,1,0:T(8,128)S(1)}, f32[16,32,128]{2,1,0:T(8,128)S(1)}, u32[]{:S(2)}, u32[]{:S(2)}) collective-permute-start(f32[16,32,128]{2,1,0:T(8,128)S(1)} %get-tuple-element.31), channel_id=1, source_target_pairs={{1,2},{2,1},{3,4},{4,3},{5,6},{6,5},{7,8},{8,7},{9,10},{10,9},{11,... | collective-permute-start | bytes 786440 | tf_op jit(solution)/shard_map/ppermute | solution.py:457
  13.8 44.9 %collective-permute-start.1 = (f32[16,32,128]{2,1,0:T(8,128)S(1)}, f32[16,32,128]{2,1,0:T(8,128)S(1)}, u32[]{:S(2)}, u32[]{:S(2)}) collective-permute-start(f32[16,32,128]{2,1,0:T(8,128)S(1)} %get-tuple-element.32), channel_id=1, source_target_pairs={{0,1},{1,0},{2,3},{3,2},{4,5},{5,4},{6,7},{7,6},{8,9},{9,8},{10,11... | collective-permute-start | bytes 786440 | tf_op jit(solution)/shard_map/ppermute | solution.py:457
  33.2 25.5 %collective-permute-start.4 = (f32[192,128]{1,0:T(8,128)S(1)}, f32[192,128]{1,0:T(8,128)S(1)}, u32[]{:S(2)}, u32[]{:S(2)}) collective-permute-start(f32[192,128]{1,0:T(8,128)S(1)} %get-tuple-element.44), channel_id=1, source_target_pairs={{1,2},{2,1},{3,4},{4,3},{5,6},{6,5},{7,8},{8,7},{9,10},{10,9},{11,... | collective-permute-start | bytes 294920 | tf_op jit(solution)/shard_map/ppermute | solution.py:457
  35.1 23.9 %collective-permute-start.5 = (f32[192,128]{1,0:T(8,128)S(1)}, f32[192,128]{1,0:T(8,128)S(1)}, u32[]{:S(2)}, u32[]{:S(2)}) collective-permute-start(f32[192,128]{1,0:T(8,128)S(1)} %get-tuple-element.45), channel_id=1, source_target_pairs={{0,1},{1,0},{2,3},{3,2},{4,5},{5,4},{6,7},{7,6},{8,9},{9,8},{10,11... | collective-permute-start | bytes 294920 | tf_op jit(solution)/shard_map/ppermute | solution.py:457

commit v2 on v1

--- a/solution.py
+++ b/solution.py
@@ -17,15 +17,15 @@
 TO_NEXT = (
     ("E", (0, 1, 2), (-3, -2, -1, 16, 17, 18, 19), 15),
     ("H", (0, 1, 2), (-3, -2, -1, 16, 17, 18), 15),
-    ("H", (0, 1, 2), (-2, -1, 15, 16, 17, 18), 14),
-    ("E", (0, 1, 2), (-1, 0, 15, 16, 17, 18), 14),
-    ("H", (0, 2), (0, 14, 15, 16, 17), 13),
+    ("H", (0, 1, 2), (-2, -1, 16, 17, 18), 14),
+    ("E", (0, 1, 2), (-1, 16, 17, 18), 14),
+    ("H", (0, 2), (16, 17), 13),
 )
 TO_PREV = (
     ("E", (0, 1, 2), (-4, -3, -2, -1, 16, 17, 18), 0),
-    ("H", (0, 1, 2), (-4, -3, -2, -1, 15, 16, 17), 0),
-    ("E", (0, 2), (-3, -2, -1, 0, 15, 16), 1),
-    ("H", (0, 1, 2), (-3, -2, -1, 0, 14, 15), 1),
+    ("H", (0, 1, 2), (-4, -3, -2, -1, 16, 17), 0),
+    ("E", (0, 2), (-3, -2, -1, 16), 1),
+    ("H", (0, 1, 2), (-3, -2, -1), 1),
 )
 CELLS_NEXT = tuple((x, 15) for x in (-3, -2, -1, 16, 17, 18)) + tuple((x, 14) for x in (-1, 16, 17))
 CELLS_PREV = tuple((x, 0) for x in (-3, -2, -1, 16, 17)) + tuple((x, 1) for x in (-2, -1))
@@ -61,7 +61,8 @@
 
 LIST_NEXT, LIST_PREV = entries(TO_NEXT), entries(TO_PREV)
 HALF = max(len(LIST_NEXT), len(LIST_PREV))
-CORNER_ROWS = -(-(2 * HALF + 2 * max(len(CELLS_NEXT), len(CELLS_PREV))) // 8) * 8
+FAR = 16 * 32
+Y_ROWS = FAR + -(-(2 * HALF + 2 * max(len(CELLS_NEXT), len(CELLS_PREV))) // 8) * 8
 
 X_LIST_NEXT, X_LIST_PREV = entries(X_TO_NEXT), entries(X_TO_PREV)
 X_HALF = max(len(X_LIST_NEXT), len(X_LIST_PREV))
@@ -167,21 +168,63 @@
     return re * cosine - im * sine, re * sine + im * cosine
 
 
-def pack_y(buf, E, H, mat, mask, rows, extra):
+def pack_y(buf, E, H, mat, mask, rows, extra, items, cells):
     for x in range(16):
-        X = x + OX
+        X, base = x + OX, 32 * x
         for p in range(2):
             for c in range(3):
-                at = 4 * (3 * p + c)
-                buf[x, at : at + 2, :] = E[p, c, X, rows : rows + 2, :]
-                buf[x, at + 2 : at + 4, :] = H[p, c, X, rows : rows + 2, :]
+                at = base + 4 * (3 * p + c)
+                buf[at : at + 2, :] = E[p, c, X, rows : rows + 2, :]
+                buf[at + 2 : at + 4, :] = H[p, c, X, rows : rows + 2, :]
         if extra is not None:
             for p in range(2):
                 for i, c in enumerate((0, 2)):
-                    at = 24 + 2 * p + i
-                    buf[x, at : at + 1, :] = H[p, c, X, extra : extra + 1, :]
-        buf[x, 28:30, :] = mat[X, rows : rows + 2, :]
-        buf[x, 30:32, :] = mask[X, rows : rows + 2, :]
+                    at = base + 24 + 2 * p + i
+                    buf[at : at + 1, :] = H[p, c, X, extra : extra + 1, :]
+        buf[base + 28 : base + 30, :] = mat[X, rows : rows + 2, :]
+        buf[base + 30 : base + 32, :] = mask[X, rows : rows + 2, :]
+
+    def put(row, value):
+        buf[FAR + row : FAR + row + 1, :] = value
+
+    pack_rows(put, E, H, mat, mask, items, cells, HALF)
+
+
+def unpack_y(buf, table, E, H, state, mat, mask, below, edge):
+    rows, extra, tile = (OY - 2, OY - 3, 0) if below else (OY + 16, None, 24)
+
+    def turn(re, im):
+        return turned(table, Y_TURN, re, im) if edge else (re, im)
+
+    for x in range(16):
+        X, base = x + OX, 32 * x
+        for c in range(3):
+            for f, field in enumerate((E, H)):
+                at = [base + 4 * (3 * p + c) + 2 * f for p in range(2)]
+                re, im = turn(buf[at[0] : at[0] + 2, :], buf[at[1] : at[1] + 2, :])
+                field[0, c, X, rows : rows + 2, :] = re
+                field[1, c, X, rows : rows + 2, :] = im
+        if extra is not None:
+            for i, c in enumerate((0, 2)):
+                at = base + 24 + i
+                re, im = turn(buf[at : at + 1, :], buf[at + 2 : at + 3, :])
+                H[0, c, X, extra : extra + 1, :] = re
+                H[1, c, X, extra : extra + 1, :] = im
+        mat[X, rows - tile : rows - tile + 2, :] = buf[base + 28 : base + 30, :]
+        mask[X, rows - tile : rows - tile + 2, :] = buf[base + 30 : base + 32, :]
+
+    def place(x, row):
+        return x + OX, ghost_row(row) + OY
+
+    unpack_rows(
+        lambda row: buf[FAR + row : FAR + row + 1, :],
+        E, H, mat, mask,
+        LIST_NEXT if below else LIST_PREV,
+        CELLS_NEXT if below else CELLS_PREV,
+        HALF, turn, place, tile,
+    )
+    for X in range(1, XW - 1):
+        set_coefficients(table, state, X, pl.ds(tile, 8), mat[X, :, :], mask[X, :, :])
 
 
 def pack_x(buf, E, H, mat, mask, first, extra, items, cells):
@@ -214,7 +257,7 @@
         put(2 * half + 2 * i + 1, mask[x + OX, row + OY : row + OY + 1, :])
 
 
-def unpack_rows(get, E, H, mat, mask, items, cells, half, turn, place):
+def unpack_rows(get, E, H, mat, mask, items, cells, half, turn, place, tile=0):
     for i, (name, c, x, row) in enumerate(items):
         field = E if name == "E" else H
         X, R = place(x, row)
@@ -223,13 +266,13 @@
         field[1, c, X, R : R + 1, :] = im
     for i, (x, row) in enumerate(cells):
         X, R = place(x, row)
-        mat[X, R : R + 1, :] = get(2 * half + 2 * i)
-        mask[X, R : R + 1, :] = get(2 * half + 2 * i + 1)
+        mat[X, R - tile : R - tile + 1, :] = get(2 * half + 2 * i)
+        mask[X, R - tile : R - tile + 1, :] = get(2 * half + 2 * i + 1)
 
 
 def first_kernel(
     e_in, h_in, mat_in, mask_in, eps_in, sigma_in, phase_in,
-    E, H, scale, drive, decay, push, mat, mask, table, xa, xb, ya, yb,
+    E, H, scale, drive, decay, push, mat, mask, table, xa, xb,
     raw_mat, raw_mask, eps, sigma, phase, sems,
 ):
     state = (scale, drive, decay, push)
@@ -275,12 +318,7 @@
         pack_x(to_next, E, H, mat, mask, 14, 13, X_LIST_NEXT, X_CELLS_NEXT)
         pack_x(to_prev, E, H, mat, mask, 0, None, X_LIST_PREV, X_CELLS_PREV)
 
-    def y_faces(to_next, to_prev):
-        pack_y(to_next, E, H, mat, mask, OY + 14, OY + 13)
-        pack_y(to_prev, E, H, mat, mask, OY, None)
-
     either(is_odd("gx"), x_faces, xa, xb)
-    either(is_odd("gy"), y_faces, ya, yb)
 
 
 def second_kernel(
@@ -343,12 +381,8 @@
     half_h(E, H, decay, push, 14, 17, own(1, 14))
 
     def pack(to_next, to_prev):
-        for buf, items, cells in ((to_next, LIST_NEXT, CELLS_NEXT), (to_prev, LIST_PREV, CELLS_PREV)):
-
-            def put(row, value, buf=buf):
-                buf[row : row + 1, :] = value
-
-            pack_rows(put, E, H, mat, mask, items, cells, HALF)
+        pack_y(to_next, E, H, mat, mask, OY + 14, OY + 13, LIST_NEXT, CELLS_NEXT)
+        pack_y(to_prev, E, H, mat, mask, OY, None, LIST_PREV, CELLS_PREV)
 
     either(is_odd("gy"), pack, ya, yb)
 
@@ -364,58 +398,26 @@
     half_e(E, H, scale, drive, 0, 16, own(4, 12))
 
 
+def fourth_kernel(
+    ya, table, e_io, h_io, s_io, d_io, c_io, p_io,
+    E, H, scale, drive, decay, push,
+    mat, mask,
+):
+    gy_odd = is_odd("gy")
+    args = (ya, table, E, H, (scale, drive, decay, push), mat, mask)
+    pl.when(gy_odd)(lambda: unpack_y(*args, True, False))
+    pl.when(jnp.logical_not(gy_odd))(lambda: unpack_y(*args, False, False))
+
+
 def last_kernel(
-    yb, ya, zb, za, table, e_io, h_io, s_io, d_io, c_io, p_io,
+    yb, table, e_io, h_io, s_io, d_io, c_io, p_io,
     e_out, h_out, E, H, scale, drive, decay, push,
     mat, mask, sems,
 ):
-    state = (scale, drive, decay, push)
-
-    def unpack_y(buf, rows, extra, edge):
-        def turn(re, im):
-            return turned(table, Y_TURN, re, im) if edge else (re, im)
-
-        for x in range(16):
-            X = x + OX
-            for c in range(3):
-                for f, field in enumerate((E, H)):
-                    re, im = (buf[x, 4 * (3 * p + c) + 2 * f : 4 * (3 * p + c) + 2 * f + 2, :] for p in range(2))
-                    re, im = turn(re, im)
-                    field[0, c, X, rows : rows + 2, :] = re
-                    field[1, c, X, rows : rows + 2, :] = im
-            if extra is not None:
-                for i, c in enumerate((0, 2)):
-                    re, im = turn(buf[x, 24 + i : 25 + i, :], buf[x, 26 + i : 27 + i, :])
-                    H[0, c, X, extra : extra + 1, :] = re
-                    H[1, c, X, extra : extra + 1, :] = im
-            mat[X, rows : rows + 2, :] = buf[x, 28:30, :]
-            mask[X, rows : rows + 2, :] = buf[x, 30:32, :]
-
-    def ghosts(above, below, above_far, below_far, odd):
-        unpack_y(below, OY - 2, OY - 3, not odd)
-        unpack_y(above, OY + 16, None, odd)
-        for buf, items, cells, edge in (
-            (below_far, LIST_NEXT, CELLS_NEXT, not odd),
-            (above_far, LIST_PREV, CELLS_PREV, odd),
-        ):
-
-            def turn(re, im, edge=edge):
-                return turned(table, Y_TURN, re, im) if edge else (re, im)
-
-            unpack_rows(
-                lambda row, buf=buf: buf[row : row + 1, :],
-                E, H, mat, mask, items, cells, HALF, turn,
-                lambda x, row: (x + OX, ghost_row(row) + OY),
-            )
-
     gy_odd = is_odd("gy")
-    pl.when(gy_odd)(lambda: ghosts(yb, ya, zb, za, True))
-    pl.when(jnp.logical_not(gy_odd))(lambda: ghosts(ya, yb, za, zb, False))
-
-    for X in range(1, XW - 1):
-        for start in (0, 24):
-            s = pl.ds(start, 8)
-            set_coefficients(table, state, X, s, mat[X, s, :], mask[X, s, :])
+    args = (yb, table, E, H, (scale, drive, decay, push), mat, mask)
+    pl.when(gy_odd)(lambda: unpack_y(*args, False, True))
+    pl.when(jnp.logical_not(gy_odd))(lambda: unpack_y(*args, True, True))
 
     def sides(low, low_end, high, high_end):
         return ((4, low, low_end), (20, high, high_end))
@@ -443,8 +445,7 @@
 CELL = jax.ShapeDtypeStruct((XW, YW, LANES), F32)
 TABLE = jax.ShapeDtypeStruct((24, LANES), F32)
 X_FACE = jax.ShapeDtypeStruct((X_SLABS, 16, LANES), F32)
-Y_FACE = jax.ShapeDtypeStruct((16, 32, LANES), F32)
-FAR_FACE = jax.ShapeDtypeStruct((CORNER_ROWS, LANES), F32)
+Y_FACE = jax.ShapeDtypeStruct((Y_ROWS, LANES), F32)
 PARAMS = pltpu.CompilerParams(vmem_limit_bytes=32 * 1024 * 1024)
 
 
@@ -460,9 +461,9 @@
 def per_device(electric, magnetic, material, absorber_mask, permittivity, conductivity, bloch_phase):
     out = pl.pallas_call(
         first_kernel,
-        out_shape=(FIELD, FIELD) + (CELL,) * 6 + (TABLE, X_FACE, X_FACE, Y_FACE, Y_FACE),
+        out_shape=(FIELD, FIELD) + (CELL,) * 6 + (TABLE, X_FACE, X_FACE),
         in_specs=[HBM] * 7,
-        out_specs=(VMEM,) * 13,
+        out_specs=(VMEM,) * 11,
         scratch_shapes=[
             pltpu.VMEM((16, 16, LANES), jnp.int32),
             pltpu.VMEM((16, 16, LANES), jnp.int32),
@@ -474,23 +475,21 @@
         compiler_params=PARAMS,
         name="first",
     )(*(pltpu.with_memory_space_constraint(v, pltpu.HBM) for v in (electric, magnetic, material, absorber_mask, permittivity, conductivity, bloch_phase)))
-    state, table, (xa, xb, ya, yb) = out[:8], out[8], out[9:]
+    state, table, (xa, xb) = out[:8], out[8], out[9:]
     xb = swapped(xb, "gx", 1)
-    yb = swapped(yb, "gy", 1)
     xa = swapped(xa, "gx", 0)
-    ya = swapped(ya, "gy", 0)
     out = pl.pallas_call(
         second_kernel,
-        out_shape=(FIELD, FIELD) + (CELL,) * 6 + (FAR_FACE, FAR_FACE),
+        out_shape=(FIELD, FIELD) + (CELL,) * 6 + (Y_FACE, Y_FACE),
         in_specs=[VMEM] * 11,
         out_specs=(VMEM,) * 10,
         input_output_aliases={3 + i: i for i in range(8)},
         compiler_params=PARAMS,
         name="second",
     )(xb, xa, table, *state)
-    state, (za, zb) = out[:6], out[8:]
-    zb = swapped(zb, "gy", 1)
-    za = swapped(za, "gy", 0)
+    state, (ya, yb) = out[:6], out[8:]
+    yb = swapped(yb, "gy", 1)
+    ya = swapped(ya, "gy", 0)
     state = pl.pallas_call(
         third_kernel,
         out_shape=(FIELD, FIELD) + (CELL,) * 4,
@@ -498,8 +497,19 @@
         out_specs=(VMEM,) * 6,
         input_output_aliases={i: i for i in range(6)},
         compiler_params=PARAMS,
+        cost_estimate=pl.CostEstimate(flops=20000000000, bytes_accessed=0, transcendentals=0),
         name="third",
     )(*state)
+    state = pl.pallas_call(
+        fourth_kernel,
+        out_shape=(FIELD, FIELD) + (CELL,) * 4,
+        in_specs=[VMEM] * 8,
+        out_specs=(VMEM,) * 6,
+        input_output_aliases={2 + i: i for i in range(6)},
+        scratch_shapes=[pltpu.VMEM((XW, 8, LANES), F32), pltpu.VMEM((XW, 8, LANES), F32)],
+        compiler_params=PARAMS,
+        name="fourth",
+    )(ya, table, *state)
     out = pl.pallas_call(
         last_kernel,
         out_shape=(
@@ -509,17 +519,17 @@
             FIELD,
         )
         + (CELL,) * 4,
-        in_specs=[VMEM] * 11,
+        in_specs=[VMEM] * 8,
         out_specs=(HBM, HBM) + (VMEM,) * 6,
-        input_output_aliases={5 + i: 2 + i for i in range(6)},
+        input_output_aliases={2 + i: 2 + i for i in range(6)},
         scratch_shapes=[
-            pltpu.VMEM(CELL.shape, F32),
-            pltpu.VMEM(CELL.shape, F32),
+            pltpu.VMEM((XW, 8, LANES), F32),
+            pltpu.VMEM((XW, 8, LANES), F32),
             pltpu.SemaphoreType.DMA((2,)),
         ],
         compiler_params=PARAMS,
         name="last",
-    )(yb, ya, zb, za, table, *state)
+    )(yb, table, *state)
     return out[0], out[1]
 
 

time: 64.3 us -> 53.9 us (0.84)
  the two profiles are of different devices: /device:TPU:2 before, /device:TPU:8 now
where the time goes in v2:
time: 53.9 us; the launch traced here: 53.6 us
  starting transfers between devices  31.5 us (58%)
  waiting for transfers between devices  10.9 us (20%)
  Pallas kernels  10.6 us (20%)
  between operations  0.69 us (1%)
    ppermute x4, starting transfers between devices, swapped(): return lax.ppermute(value, axis, pairs)  31.5 us
    ppermute x4, waiting for transfers between devices, swapped(): return lax.ppermute(value, axis, pairs)  10.9 us
    pallas_call x1, Pallas kernels, per_device(): pl.pallas_call(last_kernel, out_shape=(jax.ShapeDtypeStruct(electric.shap...  4.72 us
    pallas_call x1, Pallas kernels, per_device(): pl.pallas_call(first_kernel, out_shape=(FIELD, FIELD) + (CELL,) * 6 + (TA...  2.6 us
    pallas_call x1, Pallas kernels, per_device(): pl.pallas_call(third_kernel, out_shape=(FIELD, FIELD) + (CELL,) * 4, in_s...  2.17 us
  transfers between devices with their start and end apart: 4, of which 3 were waited for; matrix products, arithmetic and copies ran while one was open for 0% of the time, Pallas kernels for 5%

profile of v2, /device:TPU:8, one launch (start us, length us, event | category | flops | bytes accessed | tf_op | source)
XLA Modules:
  0.0 53.6 jit_solution(6656849965658096287)
XLA Ops:
  0.6 2.6 %first.1 = (f32[2,3,24,32,128]{4,3,2,1,0:T(8,128)S(1)}, f32[2,3,24,32,128]{4,3,2,1,0:T(8,128)S(1)}, f32[24,32,128]{2,1,0:T(8,128)S(1)}, f32[24,32,128]{2,1,0:T(8...) custom-call(f32[2,3,16,16,128]{4,3,2,1,0:T(8,128)} %e_in.1, ...), custom_call_target="tpu_custom_call" | custom-call | tf_op jit(solution)/shard_map/first/pallas_call | solution.py:462
  3.2 1.9 %collective-permute-start = (f32[36,16,128]{2,1,0:T(8,128)S(1)}, f32[36,16,128]{2,1,0:T(8,128)S(1)}, u32[]{:S(2)}, u32[]{:S(2)}) collective-permute-start(f32[36,16,128]{2,1,0:T(8,128)S(1)} %get-tuple-element.35), channel_id=1, source_target_pairs={{96,192},{192,96},{288,384},{384,288},{480,576},{576,480},{672,0},... | collective-permute-start | bytes 884744 | tf_op jit(solution)/shard_map/ppermute | solution.py:458
  5.2 3.6 %collective-permute-start.1 = (f32[36,16,128]{2,1,0:T(8,128)S(1)}, f32[36,16,128]{2,1,0:T(8,128)S(1)}, u32[]{:S(2)}, u32[]{:S(2)}) collective-permute-start(f32[36,16,128]{2,1,0:T(8,128)S(1)} %get-tuple-element.36), channel_id=1, source_target_pairs={{0,96},{96,0},{192,288},{288,192},{384,480},{480,384},{576,672},{6... | collective-permute-start | bytes 884744 | tf_op jit(solution)/shard_map/ppermute | solution.py:458
  8.8 2.5 %collective-permute-done.xb = f32[36,16,128]{2,1,0:T(8,128)S(1)} collective-permute-done((f32[36,16,128]{2,1,0:T(8,128)S(1)}, f32[36,16,128]{2,1,0:T(8,128)S(1)}, u32[]{:S(2)}, u32[]{:S(2)}) %collective-permute-start) | collective-permute-done | bytes 294944 | tf_op jit(solution)/shard_map/ppermute | solution.py:458
  11.3 0.0 collective-permute-done.1.xa
  11.3 0.8 %second.1 = (f32[2,3,24,32,128]{4,3,2,1,0:T(8,128)S(1)}, f32[2,3,24,32,128]{4,3,2,1,0:T(8,128)S(1)}, f32[24,32,128]{2,1,0:T(8,128)S(1)}, f32[24,32,128]{2,1,0:T(...) custom-call(f32[36,16,128]{2,1,0:T(8,128)S(1)} %collective-permute-d, ...), custom_call_target="tpu_custom_call", output_to_operand_aliasing={{0}: (3, {}), {1}: (4, {}), {2}: (5, {}), {3}: (6, {}), {4}... | custom-call | tf_op jit(solution)/shard_map/second/pallas_call | solution.py:481
  12.1 24.0 %collective-permute-start.2 = (f32[672,128]{1,0:T(8,128)S(1)}, f32[672,128]{1,0:T(8,128)S(1)}, u32[]{:S(2)}, u32[]{:S(2)}) collective-permute-start(f32[672,128]{1,0:T(8,128)S(1)} %get-tuple-element.46), channel_id=1, source_target_pairs={{1,2},{2,1},{3,4},{4,3},{5,6},{6,5},{7,8},{8,7},{9,10},{10,9},{11,... | collective-permute-start | bytes 1032200 | tf_op jit(solution)/shard_map/ppermute | solution.py:458
  36.1 1.9 %collective-permute-start.3 = (f32[672,128]{1,0:T(8,128)S(1)}, f32[672,128]{1,0:T(8,128)S(1)}, u32[]{:S(2)}, u32[]{:S(2)}) collective-permute-start(f32[672,128]{1,0:T(8,128)S(1)} %get-tuple-element.47), channel_id=1, source_target_pairs={{0,1},{1,0},{2,3},{3,2},{4,5},{5,4},{6,7},{7,6},{8,9},{9,8},{10,11... | collective-permute-start | bytes 1032200 | tf_op jit(solution)/shard_map/ppermute | solution.py:458
  38.1 2.2 %third.1 = (f32[2,3,24,32,128]{4,3,2,1,0:T(8,128)S(1)}, f32[2,3,24,32,128]{4,3,2,1,0:T(8,128)S(1)}, f32[24,32,128]{2,1,0:T(8,128)S(1)}, f32[24,32,128]{2,1,0:T(8...) custom-call(f32[2,3,24,32,128]{4,3,2,1,0:T(8,128)S(1)} %get-tuple-el, ...), custom_call_target="tpu_custom_call", output_to_operand_aliasing={{0}: (0, {}), {1}: (1, {}), {2}: (2, {}), {3}: (3, {}), {4}... | custom-call | flops 20000000000 | tf_op jit(solution)/shard_map/third/pallas_call | solution.py:493
  40.2 6.1 %collective-permute-done.3.ya = f32[672,128]{1,0:T(8,128)S(1)} collective-permute-done((f32[672,128]{1,0:T(8,128)S(1)}, f32[672,128]{1,0:T(8,128)S(1)}, u32[]{:S(2)}, u32[]{:S(2)}) %collective-permute-start.3) | collective-permute-done | bytes 344096 | tf_op jit(solution)/shard_map/ppermute | solution.py:458
  46.4 0.3 fourth.1
  46.6 2.3 %collective-permute-done.2.yb = f32[672,128]{1,0:T(8,128)S(1)} collective-permute-done((f32[672,128]{1,0:T(8,128)S(1)}, f32[672,128]{1,0:T(8,128)S(1)}, u32[]{:S(2)}, u32[]{:S(2)}) %collective-permute-start.2) | collective-permute-done | bytes 344096 | tf_op jit(solution)/shard_map/ppermute | solution.py:458
  48.9 4.7 %last.1 = (f32[2,3,16,16,128]{4,3,2,1,0:T(8,128)}, f32[2,3,16,16,128]{4,3,2,1,0:T(8,128)}, f32[2,3,24,32,128]{4,3,2,1,0:T(8,128)S(1)}, f32[2,3,24,32,128]{4,3,2,...) custom-call(f32[672,128]{1,0:T(8,128)S(1)} %collective-permute-done., ...), custom_call_target="tpu_custom_call", output_to_operand_aliasing={{2}: (2, {}), {3}: (3, {}), {4}: (4, {}), {5}: (5, {}), {6}... | custom-call | tf_op jit(solution)/shard_map/last/pallas_call | solution.py:513
Async XLA Ops:
  3.2 8.0 %collective-permute-start = (f32[36,16,128]{2,1,0:T(8,128)S(1)}, f32[36,16,128]{2,1,0:T(8,128)S(1)}, u32[]{:S(2)}, u32[]{:S(2)}) collective-permute-start(f32[36,16,128]{2,1,0:T(8,128)S(1)} %get-tuple-element.35), channel_id=1, source_target_pairs={{96,192},{192,96},{288,384},{384,288},{480,576},{576,480},{672,0},... | collective-permute-start | bytes 884744 | tf_op jit(solution)/shard_map/ppermute | solution.py:458
  5.2 6.1 %collective-permute-start.1 = (f32[36,16,128]{2,1,0:T(8,128)S(1)}, f32[36,16,128]{2,1,0:T(8,128)S(1)}, u32[]{:S(2)}, u32[]{:S(2)}) collective-permute-start(f32[36,16,128]{2,1,0:T(8,128)S(1)} %get-tuple-element.36), channel_id=1, source_target_pairs={{0,96},{96,0},{192,288},{288,192},{384,480},{480,384},{576,672},{6... | collective-permute-start | bytes 884744 | tf_op jit(solution)/shard_map/ppermute | solution.py:458
  12.1 36.8 %collective-permute-start.2 = (f32[672,128]{1,0:T(8,128)S(1)}, f32[672,128]{1,0:T(8,128)S(1)}, u32[]{:S(2)}, u32[]{:S(2)}) collective-permute-start(f32[672,128]{1,0:T(8,128)S(1)} %get-tuple-element.46), channel_id=1, source_target_pairs={{1,2},{2,1},{3,4},{4,3},{5,6},{6,5},{7,8},{8,7},{9,10},{10,9},{11,... | collective-permute-start | bytes 1032200 | tf_op jit(solution)/shard_map/ppermute | solution.py:458
  36.1 10.2 %collective-permute-start.3 = (f32[672,128]{1,0:T(8,128)S(1)}, f32[672,128]{1,0:T(8,128)S(1)}, u32[]{:S(2)}, u32[]{:S(2)}) collective-permute-start(f32[672,128]{1,0:T(8,128)S(1)} %get-tuple-element.47), channel_id=1, source_target_pairs={{0,1},{1,0},{2,3},{3,2},{4,5},{5,4},{6,7},{7,6},{8,9},{9,8},{10,11... | collective-permute-start | bytes 1032200 | tf_op jit(solution)/shard_map/ppermute | solution.py:458

commit v3 on v2

--- a/solution.py
+++ b/solution.py
@@ -92,6 +92,13 @@
 
 def half_step(field, other, keep, gain, xlow, xhigh, windows, sign):
     along_z = ahead if sign == 1 else behind
+    beside = {
+        (X, start, p, c): along_z(other[p, c, X, pl.ds(start, 8), :])
+        for X in range(xlow + OX, xhigh + OX)
+        for start, _, _ in windows
+        for p in range(2)
+        for c in (1, 0)
+    }
     for X in range(xlow + OX, xhigh + OX):
         for start, low, high in windows:
             s, n = pl.ds(start, 8), pl.ds(start + sign, 8)
@@ -102,8 +109,8 @@
                 y_x, y_z = other[p, 0, X, n, :], other[p, 2, X, n, :]
                 x_y, x_z = other[p, 1, X + sign, s, :], other[p, 2, X + sign, s, :]
                 curl = (
-                    (y_z - fz) - (along_z(fy) - fy),
-                    (along_z(fx) - fx) - (x_z - fz),
+                    (y_z - fz) - (beside[X, start, p, 1] - fy),
+                    (beside[X, start, p, 0] - fx) - (x_z - fz),
                     (x_y - fy) - (y_x - fx),
                 )
                 for c in range(3):
@@ -422,21 +429,36 @@
     def sides(low, low_end, high, high_end):
         return ((4, low, low_end), (20, high, high_end))
 
-    half_h(E, H, decay, push, -4, 19, sides(-1, 0, 15, 16))
-    half_e(E, H, scale, drive, -3, 19, sides(-1, 1, 15, 17))
-    half_h(E, H, decay, push, -3, 18, sides(-2, 1, 14, 17))
-    half_e(E, H, scale, drive, -2, 18, sides(-2, 2, 14, 18))
-    half_h(E, H, decay, push, -2, 17, sides(-2, 2, 13, 17))
-    half_e(E, H, scale, drive, -1, 17, sides(-1, 3, 13, 17))
-    half_h(E, H, decay, push, -1, 16, sides(-1, 3, 12, 16))
-    inside = (slice(None), slice(None), pl.ds(OX, 16), pl.ds(OY, 16), slice(None))
-    copy_h = pltpu.make_async_copy(H.at[inside], h_out, sems.at[0])
-    copy_h.start()
-    half_e(E, H, scale, drive, 0, 16, sides(0, 4, 12, 16))
-    copy_e = pltpu.make_async_copy(E.at[inside], e_out, sems.at[1])
-    copy_e.start()
-    copy_h.wait()
-    copy_e.wait()
+    copies = []
+    for part, (start, end) in enumerate(((None, 8), (8, 16))):
+
+        def span(low, shift, high, start=start, end=end):
+            return low if start is None else start + shift, high if end == 16 else end + shift
+
+        half_h(E, H, decay, push, *span(-4, 3, 19), sides(-1, 0, 15, 16))
+        half_e(E, H, scale, drive, *span(-3, 3, 19), sides(-1, 1, 15, 17))
+        half_h(E, H, decay, push, *span(-3, 2, 18), sides(-2, 1, 14, 17))
+        half_e(E, H, scale, drive, *span(-2, 2, 18), sides(-2, 2, 14, 18))
+        half_h(E, H, decay, push, *span(-2, 1, 17), sides(-2, 2, 13, 17))
+        half_e(E, H, scale, drive, *span(-1, 1, 17), sides(-1, 3, 13, 17))
+        half_h(E, H, decay, push, *span(-1, 0, 16), sides(-1, 3, 12, 16))
+        copies += copy_out(H, h_out, sems.at[2 * part], end - 8)
+        half_e(E, H, scale, drive, *span(0, 0, 16), sides(0, 4, 12, 16))
+        copies += copy_out(E, e_out, sems.at[2 * part + 1], end - 8)
+    for copy in copies:
+        copy.wait()
+
+
+def copy_out(field, out, sem, first):
+    copies = []
+    for p in range(2):
+        for c in range(3):
+            copy = pltpu.make_async_copy(
+                field.at[p, c, pl.ds(first + OX, 8), pl.ds(OY, 16)], out.at[p, c, pl.ds(first, 8)], sem.at[3 * p + c]
+            )
+            copy.start()
+            copies.append(copy)
+    return copies
 
 
 VMEM = pl.BlockSpec(memory_space=pltpu.VMEM)
@@ -525,7 +547,7 @@
         scratch_shapes=[
             pltpu.VMEM((XW, 8, LANES), F32),
             pltpu.VMEM((XW, 8, LANES), F32),
-            pltpu.SemaphoreType.DMA((2,)),
+            pltpu.SemaphoreType.DMA((4, 6)),
         ],
         compiler_params=PARAMS,
         name="last",

time: 53.9 us -> 52.6 us (0.976)
  Pallas kernels: 10.6 us -> 8.67 us
  waiting for transfers between devices: 10.9 us -> 11.5 us
    pallas_call x1, Pallas kernels: 4.72 us -> 3.65 us  [per_device(): pl.pallas_call(last_kernel, out_shape=(jax.ShapeDtypeStruct(electric.shap...]
    pallas_call x1, Pallas kernels: 2.17 us -> 1.55 us  [per_device(): pl.pallas_call(third_kernel, out_shape=(FIELD, FIELD) + (CELL,) * 4, in_s...]
    ppermute x4, waiting for transfers between devices: 10.9 us -> 11.5 us  [swapped(): return lax.ppermute(value, axis, pairs)]
  transfers between devices with their start and end apart: 4 -> 4, of which waited for: 3 -> 3; matrix products, arithmetic and copies ran while one was open for 0% -> 0% of each run, Pallas kernels for 5% -> 3%
where the time goes in v3:
time: 52.6 us; the launch traced here: 52.3 us
  starting transfers between devices  31.5 us (60%)
  waiting for transfers between devices  11.5 us (22%)
  Pallas kernels  8.67 us (16%)
  between operations  0.69 us (1%)
    ppermute x4, starting transfers between devices, swapped(): return lax.ppermute(value, axis, pairs)  31.5 us
    ppermute x4, waiting for transfers between devices, swapped(): return lax.ppermute(value, axis, pairs)  11.5 us
    pallas_call x1, Pallas kernels, per_device(): pl.pallas_call(last_kernel, out_shape=(jax.ShapeDtypeStruct(electric.shap...  3.65 us
    pallas_call x1, Pallas kernels, per_device(): pl.pallas_call(first_kernel, out_shape=(FIELD, FIELD) + (CELL,) * 6 + (TA...  2.42 us
    pallas_call x1, Pallas kernels, per_device(): pl.pallas_call(third_kernel, out_shape=(FIELD, FIELD) + (CELL,) * 4, in_s...  1.55 us
  transfers between devices with their start and end apart: 4, of which 3 were waited for; matrix products, arithmetic and copies ran while one was open for 0% of the time, Pallas kernels for 3%

profile of v3, /device:TPU:8, one launch (start us, length us, event | category | flops | bytes accessed | tf_op | source)
XLA Modules:
  0.0 52.3 jit_solution(8706952581227226479)
XLA Ops:
  0.6 2.4 %first.1 = (f32[2,3,24,32,128]{4,3,2,1,0:T(8,128)S(1)}, f32[2,3,24,32,128]{4,3,2,1,0:T(8,128)S(1)}, f32[24,32,128]{2,1,0:T(8,128)S(1)}, f32[24,32,128]{2,1,0:T(8...) custom-call(f32[2,3,16,16,128]{4,3,2,1,0:T(8,128)} %e_in.1, ...), custom_call_target="tpu_custom_call" | custom-call | tf_op jit(solution)/shard_map/first/pallas_call | solution.py:484
  3.1 1.9 %collective-permute-start = (f32[36,16,128]{2,1,0:T(8,128)S(1)}, f32[36,16,128]{2,1,0:T(8,128)S(1)}, u32[]{:S(2)}, u32[]{:S(2)}) collective-permute-start(f32[36,16,128]{2,1,0:T(8,128)S(1)} %get-tuple-element.35), channel_id=1, source_target_pairs={{96,192},{192,96},{288,384},{384,288},{480,576},{576,480},{672,0},... | collective-permute-start | bytes 884744 | tf_op jit(solution)/shard_map/ppermute | solution.py:480
  5.0 3.6 %collective-permute-start.1 = (f32[36,16,128]{2,1,0:T(8,128)S(1)}, f32[36,16,128]{2,1,0:T(8,128)S(1)}, u32[]{:S(2)}, u32[]{:S(2)}) collective-permute-start(f32[36,16,128]{2,1,0:T(8,128)S(1)} %get-tuple-element.36), channel_id=1, source_target_pairs={{0,96},{96,0},{192,288},{288,192},{384,480},{480,384},{576,672},{6... | collective-permute-start | bytes 884744 | tf_op jit(solution)/shard_map/ppermute | solution.py:480
  8.6 2.5 %collective-permute-done.xb = f32[36,16,128]{2,1,0:T(8,128)S(1)} collective-permute-done((f32[36,16,128]{2,1,0:T(8,128)S(1)}, f32[36,16,128]{2,1,0:T(8,128)S(1)}, u32[]{:S(2)}, u32[]{:S(2)}) %collective-permute-start) | collective-permute-done | bytes 294944 | tf_op jit(solution)/shard_map/ppermute | solution.py:480
  11.1 0.0 collective-permute-done.1.xa
  11.1 0.8 %second.1 = (f32[2,3,24,32,128]{4,3,2,1,0:T(8,128)S(1)}, f32[2,3,24,32,128]{4,3,2,1,0:T(8,128)S(1)}, f32[24,32,128]{2,1,0:T(8,128)S(1)}, f32[24,32,128]{2,1,0:T(...) custom-call(f32[36,16,128]{2,1,0:T(8,128)S(1)} %collective-permute-d, ...), custom_call_target="tpu_custom_call", output_to_operand_aliasing={{0}: (3, {}), {1}: (4, {}), {2}: (5, {}), {3}: (6, {}), {4}... | custom-call | tf_op jit(solution)/shard_map/second/pallas_call | solution.py:503
  11.9 24.1 %collective-permute-start.2 = (f32[672,128]{1,0:T(8,128)S(1)}, f32[672,128]{1,0:T(8,128)S(1)}, u32[]{:S(2)}, u32[]{:S(2)}) collective-permute-start(f32[672,128]{1,0:T(8,128)S(1)} %get-tuple-element.46), channel_id=1, source_target_pairs={{1,2},{2,1},{3,4},{4,3},{5,6},{6,5},{7,8},{8,7},{9,10},{10,9},{11,... | collective-permute-start | bytes 1032200 | tf_op jit(solution)/shard_map/ppermute | solution.py:480
  36.0 1.9 %collective-permute-start.3 = (f32[672,128]{1,0:T(8,128)S(1)}, f32[672,128]{1,0:T(8,128)S(1)}, u32[]{:S(2)}, u32[]{:S(2)}) collective-permute-start(f32[672,128]{1,0:T(8,128)S(1)} %get-tuple-element.47), channel_id=1, source_target_pairs={{0,1},{1,0},{2,3},{3,2},{4,5},{5,4},{6,7},{7,6},{8,9},{9,8},{10,11... | collective-permute-start | bytes 1032200 | tf_op jit(solution)/shard_map/ppermute | solution.py:480
  37.9 1.6 %third.1 = (f32[2,3,24,32,128]{4,3,2,1,0:T(8,128)S(1)}, f32[2,3,24,32,128]{4,3,2,1,0:T(8,128)S(1)}, f32[24,32,128]{2,1,0:T(8,128)S(1)}, f32[24,32,128]{2,1,0:T(8...) custom-call(f32[2,3,24,32,128]{4,3,2,1,0:T(8,128)S(1)} %get-tuple-el, ...), custom_call_target="tpu_custom_call", output_to_operand_aliasing={{0}: (0, {}), {1}: (1, {}), {2}: (2, {}), {3}: (3, {}), {4}... | custom-call | flops 20000000000 | tf_op jit(solution)/shard_map/third/pallas_call | solution.py:515
  39.4 6.7 %collective-permute-done.3.ya = f32[672,128]{1,0:T(8,128)S(1)} collective-permute-done((f32[672,128]{1,0:T(8,128)S(1)}, f32[672,128]{1,0:T(8,128)S(1)}, u32[]{:S(2)}, u32[]{:S(2)}) %collective-permute-start.3) | collective-permute-done | bytes 344096 | tf_op jit(solution)/shard_map/ppermute | solution.py:480
  46.2 0.3 fourth.1
  46.4 2.2 %collective-permute-done.2.yb = f32[672,128]{1,0:T(8,128)S(1)} collective-permute-done((f32[672,128]{1,0:T(8,128)S(1)}, f32[672,128]{1,0:T(8,128)S(1)}, u32[]{:S(2)}, u32[]{:S(2)}) %collective-permute-start.2) | collective-permute-done | bytes 344096 | tf_op jit(solution)/shard_map/ppermute | solution.py:480
  48.7 3.6 %last.1 = (f32[2,3,16,16,128]{4,3,2,1,0:T(8,128)}, f32[2,3,16,16,128]{4,3,2,1,0:T(8,128)}, f32[2,3,24,32,128]{4,3,2,1,0:T(8,128)S(1)}, f32[2,3,24,32,128]{4,3,2,...) custom-call(f32[672,128]{1,0:T(8,128)S(1)} %collective-permute-done., ...), custom_call_target="tpu_custom_call", output_to_operand_aliasing={{2}: (2, {}), {3}: (3, {}), {4}: (4, {}), {5}: (5, {}), {6}... | custom-call | tf_op jit(solution)/shard_map/last/pallas_call | solution.py:535
Async XLA Ops:
  3.1 8.0 %collective-permute-start = (f32[36,16,128]{2,1,0:T(8,128)S(1)}, f32[36,16,128]{2,1,0:T(8,128)S(1)}, u32[]{:S(2)}, u32[]{:S(2)}) collective-permute-start(f32[36,16,128]{2,1,0:T(8,128)S(1)} %get-tuple-element.35), channel_id=1, source_target_pairs={{96,192},{192,96},{288,384},{384,288},{480,576},{576,480},{672,0},... | collective-permute-start | bytes 884744 | tf_op jit(solution)/shard_map/ppermute | solution.py:480
  5.0 6.1 %collective-permute-start.1 = (f32[36,16,128]{2,1,0:T(8,128)S(1)}, f32[36,16,128]{2,1,0:T(8,128)S(1)}, u32[]{:S(2)}, u32[]{:S(2)}) collective-permute-start(f32[36,16,128]{2,1,0:T(8,128)S(1)} %get-tuple-element.36), channel_id=1, source_target_pairs={{0,96},{96,0},{192,288},{288,192},{384,480},{480,384},{576,672},{6... | collective-permute-start | bytes 884744 | tf_op jit(solution)/shard_map/ppermute | solution.py:480
  11.9 36.8 %collective-permute-start.2 = (f32[672,128]{1,0:T(8,128)S(1)}, f32[672,128]{1,0:T(8,128)S(1)}, u32[]{:S(2)}, u32[]{:S(2)}) collective-permute-start(f32[672,128]{1,0:T(8,128)S(1)} %get-tuple-element.46), channel_id=1, source_target_pairs={{1,2},{2,1},{3,4},{4,3},{5,6},{6,5},{7,8},{8,7},{9,10},{10,9},{11,... | collective-permute-start | bytes 1032200 | tf_op jit(solution)/shard_map/ppermute | solution.py:480
  36.0 10.2 %collective-permute-start.3 = (f32[672,128]{1,0:T(8,128)S(1)}, f32[672,128]{1,0:T(8,128)S(1)}, u32[]{:S(2)}, u32[]{:S(2)}) collective-permute-start(f32[672,128]{1,0:T(8,128)S(1)} %get-tuple-element.47), channel_id=1, source_target_pairs={{0,1},{1,0},{2,3},{3,2},{4,5},{5,4},{6,7},{7,6},{8,9},{9,8},{10,11... | collective-permute-start | bytes 1032200 | tf_op jit(solution)/shard_map/ppermute | solution.py:480

commit v4 on v3

--- a/solution.py
+++ b/solution.py
@@ -277,22 +277,55 @@
         mask[X, R - tile : R - tile + 1, :] = get(2 * half + 2 * i + 1)
 
 
+SENT_COLUMNS = (0, 1, 2, 12, 13, 14)
+
+
+def columns_of(source, field, first, count):
+    return (
+        source.at[:, :, pl.ds(first, count)],
+        field.at[:, :, pl.ds(first + OX, count), pl.ds(OY, 16)],
+    )
+
+
+def middle_kernel(
+    e_in, h_in, table, e_io, h_io, s_io, d_io, c_io, p_io, m_io, k_io,
+    E, H, scale, drive, decay, push, mat, mask,
+    sems,
+):
+    copies = [
+        pltpu.make_async_copy(*columns_of(source, field, 4, 8), sems.at[i])
+        for i, (source, field) in enumerate(((e_in, E), (h_in, H)))
+    ]
+    for copy in copies:
+        copy.start()
+    state = (scale, drive, decay, push)
+    for x in range(16):
+        if x not in SENT_COLUMNS:
+            for start in (8, 16):
+                s = pl.ds(start, 8)
+                set_coefficients(table, state, x + OX, s, mat[x + OX, s, :], mask[x + OX, s, :])
+    for copy in copies:
+        copy.wait()
+    half_h(E, H, decay, push, 3, 12, own(0, 15))
+    half_e(E, H, scale, drive, 3, 13, own(1, 15))
+    half_h(E, H, decay, push, 2, 13, own(1, 14))
+
+
 def first_kernel(
     e_in, h_in, mat_in, mask_in, eps_in, sigma_in, phase_in,
     E, H, scale, drive, decay, push, mat, mask, table, xa, xb,
     raw_mat, raw_mask, eps, sigma, phase, sems,
 ):
     state = (scale, drive, decay, push)
-    inside = (slice(None), slice(None), pl.ds(OX, 16), pl.ds(OY, 16), slice(None))
     pairs = [
         (eps_in, eps),
         (sigma_in, sigma),
         (phase_in, phase),
         (mat_in, raw_mat),
         (mask_in, raw_mask),
-        (e_in, E.at[inside]),
-        (h_in, H.at[inside]),
     ]
+    for columns in ((0, 4), (12, 4)):
+        pairs += [columns_of(e_in, E, *columns), columns_of(h_in, H, *columns)]
     copies = [pltpu.make_async_copy(a, b, sems.at[i]) for i, (a, b) in enumerate(pairs)]
     for copy in copies:
         copy.start()
@@ -313,13 +346,17 @@
             m, k = raw_mat[x, s, :].astype(F32), raw_mask[x, s, :].astype(F32)
             mat[x + OX, t, :] = m
             mask[x + OX, t, :] = k
-            set_coefficients(table, state, x + OX, t, m, k)
-    copies[5].wait()
-    copies[6].wait()
-
-    half_h(E, H, decay, push, 0, 15, own(0, 15))
-    half_e(E, H, scale, drive, 1, 15, own(1, 15))
-    half_h(E, H, decay, push, 1, 14, own(1, 14))
+            if x in SENT_COLUMNS:
+                set_coefficients(table, state, x + OX, t, m, k)
+    for copy in copies[5:]:
+        copy.wait()
+
+    for low in (0, 12):
+        half_h(E, H, decay, push, low, low + 3, own(0, 15))
+    for low in (1, 13):
+        half_e(E, H, scale, drive, low, low + 2, own(1, 15))
+    for low in (1, 13):
+        half_h(E, H, decay, push, low, low + 1, own(1, 14))
 
     def x_faces(to_next, to_prev):
         pack_x(to_next, E, H, mat, mask, 14, 13, X_LIST_NEXT, X_CELLS_NEXT)
@@ -480,7 +517,12 @@
     return lax.ppermute(value, axis, pairs)
 
 
+def in_hbm(values):
+    return tuple(pltpu.with_memory_space_constraint(v, pltpu.HBM) for v in values)
+
+
 def per_device(electric, magnetic, material, absorber_mask, permittivity, conductivity, bloch_phase):
+    electric, magnetic = in_hbm((electric, magnetic))
     out = pl.pallas_call(
         first_kernel,
         out_shape=(FIELD, FIELD) + (CELL,) * 6 + (TABLE, X_FACE, X_FACE),
@@ -492,14 +534,25 @@
             pltpu.SMEM((8,), F32),
             pltpu.SMEM((8,), F32),
             pltpu.SMEM((2,), F32),
-            pltpu.SemaphoreType.DMA((7,)),
+            pltpu.SemaphoreType.DMA((9,)),
         ],
         compiler_params=PARAMS,
         name="first",
-    )(*(pltpu.with_memory_space_constraint(v, pltpu.HBM) for v in (electric, magnetic, material, absorber_mask, permittivity, conductivity, bloch_phase)))
+    )(electric, magnetic, *in_hbm((material, absorber_mask, permittivity, conductivity, bloch_phase)))
     state, table, (xa, xb) = out[:8], out[8], out[9:]
     xb = swapped(xb, "gx", 1)
     xa = swapped(xa, "gx", 0)
+    state = pl.pallas_call(
+        middle_kernel,
+        out_shape=(FIELD, FIELD) + (CELL,) * 6,
+        in_specs=[HBM] * 2 + [VMEM] * 9,
+        out_specs=(VMEM,) * 8,
+        input_output_aliases={3 + i: i for i in range(8)},
+        scratch_shapes=[pltpu.SemaphoreType.DMA((2,))],
+        cost_estimate=pl.CostEstimate(flops=10000000000, bytes_accessed=0, transcendentals=0),
+        compiler_params=PARAMS,
+        name="middle",
+    )(electric, magnetic, table, *state)
     out = pl.pallas_call(
         second_kernel,
         out_shape=(FIELD, FIELD) + (CELL,) * 6 + (Y_FACE, Y_FACE),

time: 52.6 us -> 51.9 us (0.987)
  waiting for transfers between devices: 11.5 us -> 9.72 us
  Pallas kernels: 8.67 us -> 9.72 us
    ppermute x4, waiting for transfers between devices: 11.5 us -> 9.72 us  [swapped(): return lax.ppermute(value, axis, pairs)]
    pallas_call x0 -> x1, Pallas kernels: none -> 1.71 us  [per_device(): pl.pallas_call(middle_kernel, out_shape=(FIELD, FIELD) + (CELL,) * 6, in_...]
    pallas_call x1, Pallas kernels: 2.42 us -> 1.76 us  [per_device(): pl.pallas_call(first_kernel, out_shape=(FIELD, FIELD) + (CELL,) * 6 + (TA...]
  transfers between devices with their start and end apart: 4 -> 4, of which waited for: 3 -> 3; matrix products, arithmetic and copies ran while one was open for 0% -> 0% of each run, Pallas kernels for 3% -> 7%
where the time goes in v4:
time: 51.9 us; the launch traced here: 51.6 us
  starting transfers between devices  31.5 us (61%)
  Pallas kernels  9.72 us (19%)
  waiting for transfers between devices  9.72 us (19%)
  between operations  0.7 us (1%)
    ppermute x4, starting transfers between devices, swapped(): return lax.ppermute(value, axis, pairs)  31.5 us
    ppermute x4, waiting for transfers between devices, swapped(): return lax.ppermute(value, axis, pairs)  9.72 us
    pallas_call x1, Pallas kernels, per_device(): pl.pallas_call(last_kernel, out_shape=(jax.ShapeDtypeStruct(electric.shap...  3.65 us
    pallas_call x1, Pallas kernels, per_device(): pl.pallas_call(first_kernel, out_shape=(FIELD, FIELD) + (CELL,) * 6 + (TA...  1.76 us
    pallas_call x1, Pallas kernels, per_device(): pl.pallas_call(middle_kernel, out_shape=(FIELD, FIELD) + (CELL,) * 6, in_...  1.71 us
    pallas_call x1, Pallas kernels, per_device(): pl.pallas_call(third_kernel, out_shape=(FIELD, FIELD) + (CELL,) * 4, in_s...  1.55 us
  transfers between devices with their start and end apart: 4, of which 3 were waited for; matrix products, arithmetic and copies ran while one was open for 0% of the time, Pallas kernels for 7%

profile of v4, /device:TPU:8, one launch (start us, length us, event | category | flops | bytes accessed | tf_op | source)
XLA Modules:
  0.0 51.6 jit_solution(3799240706817899386)
XLA Ops:
  0.6 1.8 %first.1 = (f32[2,3,24,32,128]{4,3,2,1,0:T(8,128)S(1)}, f32[2,3,24,32,128]{4,3,2,1,0:T(8,128)S(1)}, f32[24,32,128]{2,1,0:T(8,128)S(1)}, f32[24,32,128]{2,1,0:T(8...) custom-call(f32[2,3,16,16,128]{4,3,2,1,0:T(8,128)} %e_in.3, ...), custom_call_target="tpu_custom_call" | custom-call | tf_op jit(solution)/shard_map/first/pallas_call | solution.py:526
  2.4 1.9 %collective-permute-start = (f32[36,16,128]{2,1,0:T(8,128)S(1)}, f32[36,16,128]{2,1,0:T(8,128)S(1)}, u32[]{:S(2)}, u32[]{:S(2)}) collective-permute-start(f32[36,16,128]{2,1,0:T(8,128)S(1)} %get-tuple-element.43), channel_id=1, source_target_pairs={{96,192},{192,96},{288,384},{384,288},{480,576},{576,480},{672,0},... | collective-permute-start | bytes 884744 | tf_op jit(solution)/shard_map/ppermute | solution.py:517
  4.3 3.6 %collective-permute-start.1 = (f32[36,16,128]{2,1,0:T(8,128)S(1)}, f32[36,16,128]{2,1,0:T(8,128)S(1)}, u32[]{:S(2)}, u32[]{:S(2)}) collective-permute-start(f32[36,16,128]{2,1,0:T(8,128)S(1)} %get-tuple-element.44), channel_id=1, source_target_pairs={{0,96},{96,0},{192,288},{288,192},{384,480},{480,384},{576,672},{6... | collective-permute-start | bytes 884744 | tf_op jit(solution)/shard_map/ppermute | solution.py:517
  7.9 1.7 %middle.1 = (f32[2,3,24,32,128]{4,3,2,1,0:T(8,128)S(1)}, f32[2,3,24,32,128]{4,3,2,1,0:T(8,128)S(1)}, f32[24,32,128]{2,1,0:T(8,128)S(1)}, f32[24,32,128]{2,1,0:T(...) custom-call(f32[2,3,16,16,128]{4,3,2,1,0:T(8,128)} %e_in.3, ...), custom_call_target="tpu_custom_call", output_to_operand_aliasing={{0}: (3, {}), {1}: (4, {}), {2}: (5, {}), {3}: (6, {}), {4}... | custom-call | flops 10000000000 | tf_op jit(solution)/shard_map/middle/pallas_call | solution.py:545
  9.6 0.8 %collective-permute-done.xb = f32[36,16,128]{2,1,0:T(8,128)S(1)} collective-permute-done((f32[36,16,128]{2,1,0:T(8,128)S(1)}, f32[36,16,128]{2,1,0:T(8,128)S(1)}, u32[]{:S(2)}, u32[]{:S(2)}) %collective-permute-start) | collective-permute-done | bytes 294944 | tf_op jit(solution)/shard_map/ppermute | solution.py:517
  10.4 0.0 collective-permute-done.1.xa
  10.4 0.8 %second.1 = (f32[2,3,24,32,128]{4,3,2,1,0:T(8,128)S(1)}, f32[2,3,24,32,128]{4,3,2,1,0:T(8,128)S(1)}, f32[24,32,128]{2,1,0:T(8,128)S(1)}, f32[24,32,128]{2,1,0:T(...) custom-call(f32[36,16,128]{2,1,0:T(8,128)S(1)} %collective-permute-d, ...), custom_call_target="tpu_custom_call", output_to_operand_aliasing={{0}: (3, {}), {1}: (4, {}), {2}: (5, {}), {3}: (6, {}), {4}... | custom-call | tf_op jit(solution)/shard_map/second/pallas_call | solution.py:556
  11.2 24.1 %collective-permute-start.2 = (f32[672,128]{1,0:T(8,128)S(1)}, f32[672,128]{1,0:T(8,128)S(1)}, u32[]{:S(2)}, u32[]{:S(2)}) collective-permute-start(f32[672,128]{1,0:T(8,128)S(1)} %get-tuple-element.62), channel_id=1, source_target_pairs={{1,2},{2,1},{3,4},{4,3},{5,6},{6,5},{7,8},{8,7},{9,10},{10,9},{11,... | collective-permute-start | bytes 1032200 | tf_op jit(solution)/shard_map/ppermute | solution.py:517
  35.3 1.9 %collective-permute-start.3 = (f32[672,128]{1,0:T(8,128)S(1)}, f32[672,128]{1,0:T(8,128)S(1)}, u32[]{:S(2)}, u32[]{:S(2)}) collective-permute-start(f32[672,128]{1,0:T(8,128)S(1)} %get-tuple-element.63), channel_id=1, source_target_pairs={{0,1},{1,0},{2,3},{3,2},{4,5},{5,4},{6,7},{7,6},{8,9},{9,8},{10,11... | collective-permute-start | bytes 1032200 | tf_op jit(solution)/shard_map/ppermute | solution.py:517
  37.2 1.6 %third.1 = (f32[2,3,24,32,128]{4,3,2,1,0:T(8,128)S(1)}, f32[2,3,24,32,128]{4,3,2,1,0:T(8,128)S(1)}, f32[24,32,128]{2,1,0:T(8,128)S(1)}, f32[24,32,128]{2,1,0:T(8...) custom-call(f32[2,3,24,32,128]{4,3,2,1,0:T(8,128)S(1)} %get-tuple-el, ...), custom_call_target="tpu_custom_call", output_to_operand_aliasing={{0}: (0, {}), {1}: (1, {}), {2}: (2, {}), {3}: (3, {}), {4}... | custom-call | flops 20000000000 | tf_op jit(solution)/shard_map/third/pallas_call | solution.py:568
  38.8 6.7 %collective-permute-done.3.ya = f32[672,128]{1,0:T(8,128)S(1)} collective-permute-done((f32[672,128]{1,0:T(8,128)S(1)}, f32[672,128]{1,0:T(8,128)S(1)}, u32[]{:S(2)}, u32[]{:S(2)}) %collective-permute-start.3) | collective-permute-done | bytes 344096 | tf_op jit(solution)/shard_map/ppermute | solution.py:517
  45.5 0.3 fourth.1
  45.8 2.2 %collective-permute-done.2.yb = f32[672,128]{1,0:T(8,128)S(1)} collective-permute-done((f32[672,128]{1,0:T(8,128)S(1)}, f32[672,128]{1,0:T(8,128)S(1)}, u32[]{:S(2)}, u32[]{:S(2)}) %collective-permute-start.2) | collective-permute-done | bytes 344096 | tf_op jit(solution)/shard_map/ppermute | solution.py:517
  48.0 3.6 %last.1 = (f32[2,3,16,16,128]{4,3,2,1,0:T(8,128)}, f32[2,3,16,16,128]{4,3,2,1,0:T(8,128)}, f32[2,3,24,32,128]{4,3,2,1,0:T(8,128)S(1)}, f32[2,3,24,32,128]{4,3,2,...) custom-call(f32[672,128]{1,0:T(8,128)S(1)} %collective-permute-done., ...), custom_call_target="tpu_custom_call", output_to_operand_aliasing={{2}: (2, {}), {3}: (3, {}), {4}: (4, {}), {5}: (5, {}), {6}... | custom-call | tf_op jit(solution)/shard_map/last/pallas_call | solution.py:588
Async XLA Ops:
  2.4 8.0 %collective-permute-start = (f32[36,16,128]{2,1,0:T(8,128)S(1)}, f32[36,16,128]{2,1,0:T(8,128)S(1)}, u32[]{:S(2)}, u32[]{:S(2)}) collective-permute-start(f32[36,16,128]{2,1,0:T(8,128)S(1)} %get-tuple-element.43), channel_id=1, source_target_pairs={{96,192},{192,96},{288,384},{384,288},{480,576},{576,480},{672,0},... | collective-permute-start | bytes 884744 | tf_op jit(solution)/shard_map/ppermute | solution.py:517
  4.3 6.1 %collective-permute-start.1 = (f32[36,16,128]{2,1,0:T(8,128)S(1)}, f32[36,16,128]{2,1,0:T(8,128)S(1)}, u32[]{:S(2)}, u32[]{:S(2)}) collective-permute-start(f32[36,16,128]{2,1,0:T(8,128)S(1)} %get-tuple-element.44), channel_id=1, source_target_pairs={{0,96},{96,0},{192,288},{288,192},{384,480},{480,384},{576,672},{6... | collective-permute-start | bytes 884744 | tf_op jit(solution)/shard_map/ppermute | solution.py:517
  11.2 36.7 %collective-permute-start.2 = (f32[672,128]{1,0:T(8,128)S(1)}, f32[672,128]{1,0:T(8,128)S(1)}, u32[]{:S(2)}, u32[]{:S(2)}) collective-permute-start(f32[672,128]{1,0:T(8,128)S(1)} %get-tuple-element.62), channel_id=1, source_target_pairs={{1,2},{2,1},{3,4},{4,3},{5,6},{6,5},{7,8},{8,7},{9,10},{10,9},{11,... | collective-permute-start | bytes 1032200 | tf_op jit(solution)/shard_map/ppermute | solution.py:517
  35.3 10.2 %collective-permute-start.3 = (f32[672,128]{1,0:T(8,128)S(1)}, f32[672,128]{1,0:T(8,128)S(1)}, u32[]{:S(2)}, u32[]{:S(2)}) collective-permute-start(f32[672,128]{1,0:T(8,128)S(1)} %get-tuple-element.63), channel_id=1, source_target_pairs={{0,1},{1,0},{2,3},{3,2},{4,5},{5,4},{6,7},{7,6},{8,9},{9,8},{10,11... | collective-permute-start | bytes 1032200 | tf_op jit(solution)/shard_map/ppermute | solution.py:517

commit v5 on v4

--- a/solution.py
+++ b/solution.py
@@ -175,8 +175,8 @@
     return re * cosine - im * sine, re * sine + im * cosine
 
 
-def pack_y(buf, E, H, mat, mask, rows, extra, items, cells):
-    for x in range(16):
+def pack_y(buf, E, H, mat, mask, rows, extra, columns):
+    for x in columns:
         X, base = x + OX, 32 * x
         for p in range(2):
             for c in range(3):
@@ -191,6 +191,8 @@
         buf[base + 28 : base + 30, :] = mat[X, rows : rows + 2, :]
         buf[base + 30 : base + 32, :] = mask[X, rows : rows + 2, :]
 
+
+def pack_far(buf, E, H, mat, mask, items, cells):
     def put(row, value):
         buf[FAR + row : FAR + row + 1, :] = value
 
@@ -289,7 +291,7 @@
 
 def middle_kernel(
     e_in, h_in, table, e_io, h_io, s_io, d_io, c_io, p_io, m_io, k_io,
-    E, H, scale, drive, decay, push, mat, mask,
+    E, H, scale, drive, decay, push, mat, mask, ya, yb,
     sems,
 ):
     copies = [
@@ -309,6 +311,12 @@
     half_h(E, H, decay, push, 3, 12, own(0, 15))
     half_e(E, H, scale, drive, 3, 13, own(1, 15))
     half_h(E, H, decay, push, 2, 13, own(1, 14))
+
+    def pack(to_next, to_prev):
+        pack_y(to_next, E, H, mat, mask, OY + 14, OY + 13, range(1, 14))
+        pack_y(to_prev, E, H, mat, mask, OY, None, range(1, 14))
+
+    either(is_odd("gy"), pack, ya, yb)
 
 
 def first_kernel(
@@ -366,7 +374,7 @@
 
 
 def second_kernel(
-    xb, xa, table, e_io, h_io, s_io, d_io, c_io, p_io, m_io, k_io,
+    xb, xa, table, e_io, h_io, s_io, d_io, c_io, p_io, m_io, k_io, ya_io, yb_io,
     E, H, scale, drive, decay, push, mat, mask, ya, yb,
 ):
     state = (scale, drive, decay, push)
@@ -425,8 +433,10 @@
     half_h(E, H, decay, push, 14, 17, own(1, 14))
 
     def pack(to_next, to_prev):
-        pack_y(to_next, E, H, mat, mask, OY + 14, OY + 13, LIST_NEXT, CELLS_NEXT)
-        pack_y(to_prev, E, H, mat, mask, OY, None, LIST_PREV, CELLS_PREV)
+        pack_y(to_next, E, H, mat, mask, OY + 14, OY + 13, (0, 14, 15))
+        pack_far(to_next, E, H, mat, mask, LIST_NEXT, CELLS_NEXT)
+        pack_y(to_prev, E, H, mat, mask, OY, None, (0, 14, 15))
+        pack_far(to_prev, E, H, mat, mask, LIST_PREV, CELLS_PREV)
 
     either(is_odd("gy"), pack, ya, yb)
 
@@ -544,9 +554,9 @@
     xa = swapped(xa, "gx", 0)
     state = pl.pallas_call(
         middle_kernel,
-        out_shape=(FIELD, FIELD) + (CELL,) * 6,
+        out_shape=(FIELD, FIELD) + (CELL,) * 6 + (Y_FACE, Y_FACE),
         in_specs=[HBM] * 2 + [VMEM] * 9,
-        out_specs=(VMEM,) * 8,
+        out_specs=(VMEM,) * 10,
         input_output_aliases={3 + i: i for i in range(8)},
         scratch_shapes=[pltpu.SemaphoreType.DMA((2,))],
         cost_estimate=pl.CostEstimate(flops=10000000000, bytes_accessed=0, transcendentals=0),
@@ -556,9 +566,9 @@
     out = pl.pallas_call(
         second_kernel,
         out_shape=(FIELD, FIELD) + (CELL,) * 6 + (Y_FACE, Y_FACE),
-        in_specs=[VMEM] * 11,
+        in_specs=[VMEM] * 13,
         out_specs=(VMEM,) * 10,
-        input_output_aliases={3 + i: i for i in range(8)},
+        input_output_aliases={3 + i: i for i in range(10)},
         compiler_params=PARAMS,
         name="second",
     )(xb, xa, table, *state)

time: 51.9 us -> 51.7 us (level)
  no operation moved by 1% of the time
where the time goes in v5:
time: 51.7 us; the launch traced here: 51.4 us
  starting transfers between devices  31.5 us (61%)
  Pallas kernels  9.71 us (19%)
  waiting for transfers between devices  9.53 us (18%)
  between operations  0.7 us (1%)
    ppermute x4, starting transfers between devices, swapped(): return lax.ppermute(value, axis, pairs)  31.5 us
    ppermute x4, waiting for transfers between devices, swapped(): return lax.ppermute(value, axis, pairs)  9.53 us
    pallas_call x1, Pallas kernels, per_device(): pl.pallas_call(last_kernel, out_shape=(jax.ShapeDtypeStruct(electric.shap...  3.65 us
    pallas_call x1, Pallas kernels, per_device(): pl.pallas_call(middle_kernel, out_shape=(FIELD, FIELD) + (CELL,) * 6 + (Y...  1.89 us
    pallas_call x1, Pallas kernels, per_device(): pl.pallas_call(first_kernel, out_shape=(FIELD, FIELD) + (CELL,) * 6 + (TA...  1.76 us
    pallas_call x1, Pallas kernels, per_device(): pl.pallas_call(third_kernel, out_shape=(FIELD, FIELD) + (CELL,) * 4, in_s...  1.55 us
  transfers between devices with their start and end apart: 4, of which 3 were waited for; matrix products, arithmetic and copies ran while one was open for 0% of the time, Pallas kernels for 7%

profile of v5, /device:TPU:8, one launch (start us, length us, event | category | flops | bytes accessed | tf_op | source)
XLA Modules:
  0.0 51.4 jit_solution(369652807640342177)
XLA Ops:
  0.6 1.8 %first.1 = (f32[2,3,24,32,128]{4,3,2,1,0:T(8,128)S(1)}, f32[2,3,24,32,128]{4,3,2,1,0:T(8,128)S(1)}, f32[24,32,128]{2,1,0:T(8,128)S(1)}, f32[24,32,128]{2,1,0:T(8...) custom-call(f32[2,3,16,16,128]{4,3,2,1,0:T(8,128)} %e_in.3, ...), custom_call_target="tpu_custom_call" | custom-call | tf_op jit(solution)/shard_map/first/pallas_call | solution.py:536
  2.4 1.9 %collective-permute-start = (f32[36,16,128]{2,1,0:T(8,128)S(1)}, f32[36,16,128]{2,1,0:T(8,128)S(1)}, u32[]{:S(2)}, u32[]{:S(2)}) collective-permute-start(f32[36,16,128]{2,1,0:T(8,128)S(1)} %get-tuple-element.45), channel_id=1, source_target_pairs={{96,192},{192,96},{288,384},{384,288},{480,576},{576,480},{672,0},... | collective-permute-start | bytes 884744 | tf_op jit(solution)/shard_map/ppermute | solution.py:527
  4.3 3.6 %collective-permute-start.1 = (f32[36,16,128]{2,1,0:T(8,128)S(1)}, f32[36,16,128]{2,1,0:T(8,128)S(1)}, u32[]{:S(2)}, u32[]{:S(2)}) collective-permute-start(f32[36,16,128]{2,1,0:T(8,128)S(1)} %get-tuple-element.46), channel_id=1, source_target_pairs={{0,96},{96,0},{192,288},{288,192},{384,480},{480,384},{576,672},{6... | collective-permute-start | bytes 884744 | tf_op jit(solution)/shard_map/ppermute | solution.py:527
  7.9 1.9 %middle.1 = (f32[2,3,24,32,128]{4,3,2,1,0:T(8,128)S(1)}, f32[2,3,24,32,128]{4,3,2,1,0:T(8,128)S(1)}, f32[24,32,128]{2,1,0:T(8,128)S(1)}, f32[24,32,128]{2,1,0:T(...) custom-call(f32[2,3,16,16,128]{4,3,2,1,0:T(8,128)} %e_in.3, ...), custom_call_target="tpu_custom_call", output_to_operand_aliasing={{0}: (3, {}), {1}: (4, {}), {2}: (5, {}), {3}: (6, {}), {4}... | custom-call | flops 10000000000 | tf_op jit(solution)/shard_map/middle/pallas_call | solution.py:555
  9.8 0.6 %collective-permute-done.xb = f32[36,16,128]{2,1,0:T(8,128)S(1)} collective-permute-done((f32[36,16,128]{2,1,0:T(8,128)S(1)}, f32[36,16,128]{2,1,0:T(8,128)S(1)}, u32[]{:S(2)}, u32[]{:S(2)}) %collective-permute-start) | collective-permute-done | bytes 294944 | tf_op jit(solution)/shard_map/ppermute | solution.py:527
  10.4 0.0 collective-permute-done.1.xa
  10.4 0.6 %second.1 = (f32[2,3,24,32,128]{4,3,2,1,0:T(8,128)S(1)}, f32[2,3,24,32,128]{4,3,2,1,0:T(8,128)S(1)}, f32[24,32,128]{2,1,0:T(8,128)S(1)}, f32[24,32,128]{2,1,0:T(...) custom-call(f32[36,16,128]{2,1,0:T(8,128)S(1)} %collective-permute-d, ...), custom_call_target="tpu_custom_call", output_to_operand_aliasing={{0}: (3, {}), {1}: (4, {}), {2}: (5, {}), {3}: (6, {}), {4}... | custom-call | tf_op jit(solution)/shard_map/second/pallas_call | solution.py:566
  11.0 24.1 %collective-permute-start.2 = (f32[672,128]{1,0:T(8,128)S(1)}, f32[672,128]{1,0:T(8,128)S(1)}, u32[]{:S(2)}, u32[]{:S(2)}) collective-permute-start(f32[672,128]{1,0:T(8,128)S(1)} %get-tuple-element.66), channel_id=1, source_target_pairs={{1,2},{2,1},{3,4},{4,3},{5,6},{6,5},{7,8},{8,7},{9,10},{10,9},{11,... | collective-permute-start | bytes 1032200 | tf_op jit(solution)/shard_map/ppermute | solution.py:527
  35.1 1.9 %collective-permute-start.3 = (f32[672,128]{1,0:T(8,128)S(1)}, f32[672,128]{1,0:T(8,128)S(1)}, u32[]{:S(2)}, u32[]{:S(2)}) collective-permute-start(f32[672,128]{1,0:T(8,128)S(1)} %get-tuple-element.67), channel_id=1, source_target_pairs={{0,1},{1,0},{2,3},{3,2},{4,5},{5,4},{6,7},{7,6},{8,9},{9,8},{10,11... | collective-permute-start | bytes 1032200 | tf_op jit(solution)/shard_map/ppermute | solution.py:527
  37.0 1.6 %third.1 = (f32[2,3,24,32,128]{4,3,2,1,0:T(8,128)S(1)}, f32[2,3,24,32,128]{4,3,2,1,0:T(8,128)S(1)}, f32[24,32,128]{2,1,0:T(8,128)S(1)}, f32[24,32,128]{2,1,0:T(8...) custom-call(f32[2,3,24,32,128]{4,3,2,1,0:T(8,128)S(1)} %get-tuple-el, ...), custom_call_target="tpu_custom_call", output_to_operand_aliasing={{0}: (0, {}), {1}: (1, {}), {2}: (2, {}), {3}: (3, {}), {4}... | custom-call | flops 20000000000 | tf_op jit(solution)/shard_map/third/pallas_call | solution.py:578
  38.6 6.7 %collective-permute-done.3.ya = f32[672,128]{1,0:T(8,128)S(1)} collective-permute-done((f32[672,128]{1,0:T(8,128)S(1)}, f32[672,128]{1,0:T(8,128)S(1)}, u32[]{:S(2)}, u32[]{:S(2)}) %collective-permute-start.3) | collective-permute-done | bytes 344096 | tf_op jit(solution)/shard_map/ppermute | solution.py:527
  45.3 0.3 fourth.1
  45.6 2.2 %collective-permute-done.2.yb = f32[672,128]{1,0:T(8,128)S(1)} collective-permute-done((f32[672,128]{1,0:T(8,128)S(1)}, f32[672,128]{1,0:T(8,128)S(1)}, u32[]{:S(2)}, u32[]{:S(2)}) %collective-permute-start.2) | collective-permute-done | bytes 344096 | tf_op jit(solution)/shard_map/ppermute | solution.py:527
  47.8 3.6 %last.1 = (f32[2,3,16,16,128]{4,3,2,1,0:T(8,128)}, f32[2,3,16,16,128]{4,3,2,1,0:T(8,128)}, f32[2,3,24,32,128]{4,3,2,1,0:T(8,128)S(1)}, f32[2,3,24,32,128]{4,3,2,...) custom-call(f32[672,128]{1,0:T(8,128)S(1)} %collective-permute-done., ...), custom_call_target="tpu_custom_call", output_to_operand_aliasing={{2}: (2, {}), {3}: (3, {}), {4}: (4, {}), {5}: (5, {}), {6}... | custom-call | tf_op jit(solution)/shard_map/last/pallas_call | solution.py:598
Async XLA Ops:
  2.4 8.0 %collective-permute-start = (f32[36,16,128]{2,1,0:T(8,128)S(1)}, f32[36,16,128]{2,1,0:T(8,128)S(1)}, u32[]{:S(2)}, u32[]{:S(2)}) collective-permute-start(f32[36,16,128]{2,1,0:T(8,128)S(1)} %get-tuple-element.45), channel_id=1, source_target_pairs={{96,192},{192,96},{288,384},{384,288},{480,576},{576,480},{672,0},... | collective-permute-start | bytes 884744 | tf_op jit(solution)/shard_map/ppermute | solution.py:527
  4.3 6.1 %collective-permute-start.1 = (f32[36,16,128]{2,1,0:T(8,128)S(1)}, f32[36,16,128]{2,1,0:T(8,128)S(1)}, u32[]{:S(2)}, u32[]{:S(2)}) collective-permute-start(f32[36,16,128]{2,1,0:T(8,128)S(1)} %get-tuple-element.46), channel_id=1, source_target_pairs={{0,96},{96,0},{192,288},{288,192},{384,480},{480,384},{576,672},{6... | collective-permute-start | bytes 884744 | tf_op jit(solution)/shard_map/ppermute | solution.py:527
  11.0 36.7 %collective-permute-start.2 = (f32[672,128]{1,0:T(8,128)S(1)}, f32[672,128]{1,0:T(8,128)S(1)}, u32[]{:S(2)}, u32[]{:S(2)}) collective-permute-start(f32[672,128]{1,0:T(8,128)S(1)} %get-tuple-element.66), channel_id=1, source_target_pairs={{1,2},{2,1},{3,4},{4,3},{5,6},{6,5},{7,8},{8,7},{9,10},{10,9},{11,... | collective-permute-start | bytes 1032200 | tf_op jit(solution)/shard_map/ppermute | solution.py:527
  35.1 10.2 %collective-permute-start.3 = (f32[672,128]{1,0:T(8,128)S(1)}, f32[672,128]{1,0:T(8,128)S(1)}, u32[]{:S(2)}, u32[]{:S(2)}) collective-permute-start(f32[672,128]{1,0:T(8,128)S(1)} %get-tuple-element.67), channel_id=1, source_target_pairs={{0,1},{1,0},{2,3},{3,2},{4,5},{5,4},{6,7},{7,6},{8,9},{9,8},{10,11... | collective-permute-start | bytes 1032200 | tf_op jit(solution)/shard_map/ppermute | solution.py:527
